TPU v7x, 32 devices: a whole 2x2x4 slice. The times are simulated.
32 devices in a mesh: seq: 16 (over z, y, x), batch: 2 (over core).
Axes of the slice: x: 2, y: 2, z: 4, core: 2. Of those that a mesh axis runs over, the one named last changes fastest.
Arguments:
- block_input: float32 [2, 4096, 768], P('batch', 'seq'), may hold values from -6 to 6
- ln1_gain: float32 [768], replicated, may hold values from 0.5 to 1.5
- ln1_bias: float32 [768], replicated, may hold values from -0.5 to 0.5
- w_qkv: bfloat16 [768, 2304], replicated, may hold values from -0.3125 to 0.3125
- w_out: bfloat16 [768, 768], replicated, may hold values from -0.875 to 0.875
- ln2_gain: float32 [768], replicated, may hold values from 0.5 to 1.5
- ln2_bias: float32 [768], replicated, may hold values from -0.5 to 0.5
- w_up: bfloat16 [768, 3072], replicated, may hold values from -0.21875 to 0.21875
- w_down: bfloat16 [3072, 768], replicated, may hold values from -0.109375 to 0.109375
- length_draw: int32 [2], P('batch'), may hold values from 0 to 16383
- threshold_index: int32 [1], replicated, may hold values from 0 to 255
- grad_out: float32 [2, 4096, 768], P('batch', 'seq'), may hold values from -6 to 6
Outputs:
- layer_out: float32 [2, 4096, 768], P('batch', 'seq')
- grad_x: float32 [2, 4096, 768], P('batch', 'seq')
- grad_ln1_gain: float32 [768], replicated
- grad_ln1_bias: float32 [768], replicated
- grad_w_qkv: float32 [768, 2304], replicated
- grad_w_out: float32 [768, 768], replicated
- grad_ln2_gain: float32 [768], replicated
- grad_ln2_bias: float32 [768], replicated
- grad_w_up: float32 [768, 3072], replicated
- grad_w_down: float32 [3072, 768], replicated
- pruned_share: float32 [1], replicated
Inputs may be any that keep to these rules, and one draw needn't show every extreme that they name: Group g holds one sequence of 3841 + (length_draw[g] mod 256) tokens from its first slot; the other slots are padding. The threshold is threshold_index / 128.
All inputs are finite; a program needn't handle non-finite values.
Results may differ from a plain program's by a relative error of at most 0.012.
The roundings to bfloat16 on the way count: a program that leaves them out, or rounds other values in their place, can miss the bound.
Values may be sent and summed in bfloat16 or wider, within the bound.
A program may use at most 512 MiB of HBM per device.

v0:
```python
import jax
import jax.numpy as jnp
from jax import lax
from jax.sharding import PartitionSpec as P

HEADS = 12
HEAD_DIM = 64


epsilon = 1e-05
negative = -1e30
select_scale = 3.0


def prefix(shard, axis, combine, identity):
    devices, position = (lax.axis_size(axis), lax.axis_index(axis))
    everything = lax.all_gather(shard, axis)
    start = jnp.broadcast_to(jnp.asarray(identity, shard.dtype), shard.shape)

    def lap(k, before):
        reached = k < position
        new = combine(before, everything[k])
        return jnp.where(reached, new, before)

    return lax.fori_loop(0, devices, lap, start)


def entering(shard, axis, join, neutral):
    count = lax.axis_size(axis)
    place = lax.axis_index(axis)
    ahead = count - 1 - place
    gathered = lax.all_gather(
        shard.astype(jnp.bfloat16 if shard.dtype == jnp.float32 else shard.dtype), axis
    )
    state = jnp.zeros_like(shard) + jnp.asarray(neutral, shard.dtype)

    def one(lap, state):
        source = count - 1 - lap
        return join(state, lax.dynamic_index_in_dim(gathered, source, 0, False).astype(shard.dtype))

    return lax.fori_loop(0, ahead, one, state)


def layer_norm(values, norm_gain, norm_bias):
    row_mean = jnp.mean(values, axis=-1, keepdims=True)
    centred = values - row_mean
    variance = jnp.mean(centred * centred, axis=-1, keepdims=True)
    return centred * lax.rsqrt(variance + epsilon) * norm_gain + norm_bias


def gelu_tanh(values):
    return jax.nn.gelu(values, approximate=True)


def contract_rows(left_op, right_op):
    return lax.dot_general(
        left_op, right_op, (((0,), (0,)), ((), ())), preferred_element_type=jnp.float32
    )


def contract_cols(left_op, right_op):
    return lax.dot_general(
        left_op, right_op, (((1,), (1,)), ((), ())), preferred_element_type=jnp.float32
    )


def add_vectors(earlier, latter):
    return earlier + latter


def per_device(
    block_input,
    ln1_gain,
    ln1_bias,
    w_qkv,
    w_out,
    ln2_gain,
    ln2_bias,
    w_up,
    w_down,
    length_draw,
    threshold_index,
    grad_out,
):
    row_count = block_input.shape[1]
    model_width = block_input.shape[2]
    score_scale = HEAD_DIM ** (-0.5)
    seq_count = lax.axis_size("seq")
    group_len = seq_count * row_count
    device_index = lax.axis_index("seq")
    first_row = device_index * row_count
    length = group_len - row_count + 1 + length_draw[0] % row_count
    query_pos = first_row + jnp.arange(row_count, dtype=jnp.int32)
    key_pos = jnp.arange(group_len, dtype=jnp.int32)
    query_valid = query_pos < length
    key_valid = key_pos < length
    diagonal = key_pos[None, :] == query_pos[:, None]
    allowed = (key_pos[None, :] <= query_pos[:, None]) & (key_valid[None, :] | diagonal)
    chosen = (
        (key_pos[None, :] < query_pos[:, None]) & (key_pos[None, :] >= 1) & query_valid[:, None]
    )
    threshold = threshold_index[0].astype(jnp.float32) / 128.0
    row_valid = query_valid[:, None]
    zero_vector = jnp.zeros((group_len,), jnp.float32)
    zero_row = jnp.zeros((1, group_len), jnp.float32)
    tokens = block_input[0]
    normed, ln1_pull = jax.vjp(layer_norm, tokens, ln1_gain, ln1_bias)
    normed_low = normed.astype(jnp.bfloat16)
    projected = jnp.dot(normed_low, w_qkv, preferred_element_type=jnp.float32).astype(jnp.bfloat16)
    window = lax.all_gather(projected[:, model_width:], "seq", axis=0, tiled=True)
    query_heads = jnp.moveaxis(projected[:, :model_width].reshape(row_count, HEADS, HEAD_DIM), 1, 0)

    def key_of(head):
        return lax.dynamic_slice_in_dim(window, head * HEAD_DIM, HEAD_DIM, 1)

    def value_of(head):
        return lax.dynamic_slice_in_dim(window, model_width + head * HEAD_DIM, HEAD_DIM, 1)

    def head_scores(query_head, key_head):
        return contract_cols(query_head, key_head) * score_scale

    first_scores = head_scores(query_heads[0], key_of(0))
    selection = select_scale / group_len * jnp.where(chosen, jnp.maximum(first_scores, 0.0), 0.0)
    column_total = jnp.sum(selection, axis=0)
    before = prefix(column_total, "seq", add_vectors, zero_vector)
    running = jnp.cumsum(selection, axis=0)
    carried = before[None, :] + jnp.concatenate([zero_row, running[:-1]], axis=0)

    def attend(scores, value_head):
        logits = jnp.where(allowed, scores - carried, negative)
        row_peak = jnp.max(logits, axis=1, keepdims=True)
        exp_terms = jnp.exp(logits - row_peak)
        row_mass = jnp.sum(exp_terms, axis=1, keepdims=True)
        prob_low = (exp_terms / row_mass).astype(jnp.bfloat16)
        return (
            jnp.dot(prob_low, value_head, preferred_element_type=jnp.float32),
            (row_peak + jnp.log(row_mass))[:, 0],
        )

    def attend_head(head):
        return attend(head_scores(query_heads[head], key_of(head)), value_of(head))

    out_first, mass_first = attend(first_scores, value_of(0))
    out_rest, mass_rest = lax.map(attend_head, jnp.arange(1, HEADS, dtype=jnp.int32))
    head_out = jnp.concatenate([out_first[None], out_rest], axis=0)
    log_mass = jnp.concatenate([mass_first[None], mass_rest], axis=0)
    attn_mixed = jnp.where(
        row_valid, jnp.moveaxis(head_out, 0, 1).reshape(row_count, model_width), 0.0
    ).astype(jnp.bfloat16)
    residual = tokens + jnp.dot(attn_mixed, w_out, preferred_element_type=jnp.float32)
    normed_two, ln2_pull = jax.vjp(layer_norm, residual, ln2_gain, ln2_bias)
    normed_two_low = normed_two.astype(jnp.bfloat16)
    hidden = jnp.dot(normed_two_low, w_up, preferred_element_type=jnp.float32)
    activated, gelu_pull = jax.vjp(gelu_tanh, hidden)
    activated_low = activated.astype(jnp.bfloat16)
    layer_out = residual + jnp.dot(activated_low, w_down, preferred_element_type=jnp.float32)
    numerator = jnp.sum(jnp.where(chosen, jnp.clip(carried - threshold, 0.0, 1.0), 0.0))
    pair_count = jnp.sum(chosen.astype(jnp.float32))
    grad_top = grad_out[0]
    grad_top_low = grad_top.astype(jnp.bfloat16)
    grad_w_down = contract_rows(activated_low, grad_top_low)
    grad_hidden_low = gelu_pull(contract_cols(grad_top_low, w_down))[0].astype(jnp.bfloat16)
    grad_w_up = contract_rows(normed_two_low, grad_hidden_low)
    grad_resid_norm, grad_ln2_gain, grad_ln2_bias = ln2_pull(contract_cols(grad_hidden_low, w_up))
    grad_resid = grad_top + grad_resid_norm
    grad_attn_low = grad_resid.astype(jnp.bfloat16)
    grad_w_out = contract_rows(attn_mixed, grad_attn_low)
    grad_mixed = jnp.where(
        row_valid,
        contract_cols(grad_attn_low, w_out).astype(jnp.bfloat16),
        jnp.zeros((), jnp.bfloat16),
    )
    grad_heads = jnp.moveaxis(grad_mixed.reshape(row_count, HEADS, HEAD_DIM), 1, 0)

    def soften(scores, mass_head, value_head, grad_head):
        logits = jnp.where(allowed, scores - carried, negative)
        soft_probs = jnp.exp(logits - mass_head[:, None])
        grad_value = contract_rows(soft_probs.astype(jnp.bfloat16), grad_head)
        grad_prob = contract_cols(grad_head, value_head)
        row_inner = jnp.sum(soft_probs * grad_prob, axis=1, keepdims=True)
        return (soft_probs * (grad_prob - row_inner), grad_value)

    def back_head(state, head):
        running_grad, kv_store = state
        key_head = key_of(head)
        query_head = query_heads[head]
        grad_scores, grad_value = soften(
            head_scores(query_head, key_head), log_mass[head], value_of(head), grad_heads[head]
        )
        grad_low = grad_scores.astype(jnp.bfloat16)
        grad_query = jnp.dot(grad_low, key_head, preferred_element_type=jnp.float32) * score_scale
        grad_key = contract_rows(grad_low, query_head) * score_scale
        kv_store = lax.dynamic_update_slice(
            kv_store, jnp.concatenate([grad_key, grad_value], axis=1)[None], (head, 0, 0)
        )
        return ((running_grad - grad_scores, kv_store), grad_query)

    kv_empty = jnp.zeros((HEADS, group_len, 2 * HEAD_DIM), jnp.float32)
    grad_first, grad_value_first = soften(first_scores, log_mass[0], value_of(0), grad_heads[0])
    (grad_carried, kv_store), query_rest = lax.scan(
        back_head, (-grad_first, kv_empty), jnp.arange(1, HEADS, dtype=jnp.int32)
    )
    grad_column = jnp.sum(grad_carried, axis=0)
    after = entering(grad_column, "seq", add_vectors, zero_vector)
    later_rows = jnp.cumsum(grad_carried[::-1], axis=0)[::-1]
    grad_select = after[None, :] + jnp.concatenate([later_rows[1:], zero_row], axis=0)
    grad_first_low = (
        grad_first
        + select_scale / group_len * jnp.where(chosen & (first_scores > 0.0), grad_select, 0.0)
    ).astype(jnp.bfloat16)
    query_first = (
        jnp.dot(grad_first_low, key_of(0), preferred_element_type=jnp.float32) * score_scale
    )
    key_first = contract_rows(grad_first_low, query_heads[0]) * score_scale
    kv_store = lax.dynamic_update_slice(
        kv_store, jnp.concatenate([key_first, grad_value_first], axis=1)[None], (0, 0, 0)
    )
    kv_own = jnp.moveaxis(lax.psum_scatter(kv_store, "seq", scatter_dimension=1, tiled=True), 0, 1)
    grad_key = kv_own[:, :, :HEAD_DIM].reshape(row_count, model_width)
    grad_value = kv_own[:, :, HEAD_DIM:].reshape(row_count, model_width)
    grad_query = jnp.moveaxis(
        jnp.concatenate([query_first[None], query_rest], axis=0), 0, 1
    ).reshape(row_count, model_width)
    grad_qkv_low = jnp.concatenate([grad_query, grad_key, grad_value], axis=1).astype(jnp.bfloat16)
    grad_w_qkv = contract_rows(normed_low, grad_qkv_low)
    grad_tokens_norm, grad_ln1_gain, grad_ln1_bias = ln1_pull(contract_cols(grad_qkv_low, w_qkv))
    grad_x = grad_resid + grad_tokens_norm
    (
        grad_w_qkv,
        grad_w_out,
        grad_ln1_gain,
        grad_ln1_bias,
        grad_w_up,
        grad_w_down,
        grad_ln2_gain,
        grad_ln2_bias,
        numerator,
        pair_count,
    ) = lax.psum(
        (
            grad_w_qkv,
            grad_w_out,
            grad_ln1_gain,
            grad_ln1_bias,
            grad_w_up,
            grad_w_down,
            grad_ln2_gain,
            grad_ln2_bias,
            numerator,
            pair_count,
        ),
        ("seq", "batch"),
    )
    pruned_share = (numerator / pair_count).reshape(1)
    return (
        layer_out[None],
        grad_x[None],
        grad_ln1_gain,
        grad_ln1_bias,
        grad_w_qkv,
        grad_w_out,
        grad_ln2_gain,
        grad_ln2_bias,
        grad_w_up,
        grad_w_down,
        pruned_share,
    )


def solution(mesh):
    placed = (
        P("batch", "seq", None),
        P(),
        P(),
        P(),
        P(),
        P(),
        P(),
        P(),
        P(),
        P("batch"),
        P(),
        P("batch", "seq", None),
    )
    return jax.shard_map(
        per_device,
        mesh=mesh,
        in_specs=placed,
        out_specs=(
            P("batch", "seq", None),
            P("batch", "seq", None),
            P(),
            P(),
            P(),
            P(),
            P(),
            P(),
            P(),
            P(),
            P(),
        ),
        check_vma=False,
    )
```

profile of v0, /device:TPU:0, one launch (start us, length us, event | category | flops | bytes accessed | tf_op | source)
XLA Modules:
  0.0 1775.5 jit_solution(15498019651085656166)
XLA Ops:
  23.3 146.5 %all-gather.4.cloned.1.call-done = bf16[4096,1536]{1,0:T(8,128)(2,1)} async-done(((bf16[256,1536]{1,0:T(8,128)(2,1)}), bf16[4096,1536]{1,0:T(8,128)(2,1)}) %all-gather.4.cloned.1.call-update) | async-done | bytes 12582928 | tf_op jit(solution)/shard_map/all_gather | solution.py:110
  169.8 5.1 fusion.48
  191.3 41.8 %all-gather = f32[65536]{0:T(1024)} all-gather(f32[4096]{0:T(1024)S(1)} %multiply_reduce_fusion.2), channel_id=2, replica_groups=mesh['seq'=16,'batch'=2] {'seq'}, dimensions={0}, use_global_device_ids=true | all-gather | bytes 278528 | tf_op jit(solution)/shard_map/all_gather | solution.py:17
  234.8 35.5 %while.61 = (s32[]{:T(128)}, f32[4096]{0:T(1024)}, s32[]{:T(128)}, f32[16,4096]{1,0:T(8,128)}, s32[]{:T(128)}, /*index=5*/s32[]{:T(128)}) while((s32[]{:T(128)}, f32[4096]{0:T(1024)}, s32[]{:T(128)}, f32[16,4096]{1,0:T(8,128)}, s32[]{:T(128)}, /*index=5*/s32[]{:T(128)}) %tuple.134), condition=%wide.region_4.5_spmd.clone, body=%wide.region_3.4_spmd.clone.sunk | while | flops 12292 | bytes 82013 | solution.py:25
  281.5 193.3 %while.59 = (s32[]{:T(128)}, bf16[11,256,64]{1,2,0:T(8,128)(2,1)}, f32[11,256]{1,0:T(8,128)}, s32[11]{0:T(128)}, bf16[12,256,64]{2,1,0:T(8,128)(2,1)}, /*index=5...) while((s32[]{:T(128)}, bf16[11,256,64]{1,2,0:T(8,128)(2,1)}, ...), condition=%wide.region_12.13_spmd.clone, body=%wide.region_9.12_spmd.clone.sunk | while | flops 282066688 | bytes 35802980 | solution.py:144
  510.6 11.5 broadcast_in_dim.137
  522.8 270.7 %while.60 = (s32[]{:T(128)}, f32[256,4096]{1,0:T(8,128)}, f32[12,4096,128]{1,2,0:T(8,128)}, bf16[11,256,64]{1,2,0:T(8,128)(2,1)}, s32[11]{0:T(128)}, /*index=5*/...) while((s32[]{:T(128)}, f32[256,4096]{1,0:T(8,128)}, ...), condition=%wide.region_20.21_spmd.clone, body=%wide.region_18.20_spmd.clone.sunk | while | flops 687619840 | bytes 104082336 | solution.py:200
  531.5 6.7 multiply_reduce_fusion.10
  556.1 6.7 multiply_reduce_fusion.10
  580.7 6.7 multiply_reduce_fusion.10
  605.3 6.7 multiply_reduce_fusion.10
  629.9 6.7 multiply_reduce_fusion.10
  654.6 6.7 multiply_reduce_fusion.10
  679.1 6.7 multiply_reduce_fusion.10
  703.7 6.7 multiply_reduce_fusion.10
  728.3 6.7 multiply_reduce_fusion.10
  752.9 6.7 multiply_reduce_fusion.10
  777.4 6.7 multiply_reduce_fusion.10
  793.5 32.5 %rev.4 = f32[256,4096]{1,0:T(8,128)} reverse(f32[256,4096]{1,0:T(8,128)} %get-tuple-element.390), dimensions={0} | reverse | bytes 8388608 | tf_op jit(solution)/shard_map/rev | solution.py:205
  826.0 8.3 fusion.49
  846.3 33.2 %slice.52 = f32[255,4096]{1,0:T(8,128)} reverse(f32[255,4096]{1,0:T(8,128)} %bitcast.203), dimensions={0} | reverse | bytes 8355840 | tf_op jit(solution)/shard_map/slice | solution.py:206
  881.9 38.5 %all-gather.1 = bf16[65536]{0:T(1024)(128)(2,1)} all-gather(bf16[4096]{0:T(1024)(128)(2,1)S(1)} %reduce_sum.227), channel_id=3, replica_groups=mesh['seq'=16,'batch'=2] {'seq'}, dimensions={0}, use_global_device_ids=true | all-gather | bytes 139264 | tf_op jit(solution)/shard_map/all_gather | solution.py:32
  922.0 13.5 while.58
  935.5 7.7 add_convert_fusion
  954.1 5.3 fusion.95
  959.5 6.0 fusion.85
  965.4 341.1 %reduce-scatter.2.cloned.1.call-done = f32[12,256,128]{1,2,0:T(8,128)} async-done(((f32[12,4096,128]{1,2,0:T(8,128)}), f32[12,256,128]{1,2,0:T(8,128)}) %reduce-scatter.2.cloned.1.call-update) | async-done | bytes 1572880 | tf_op jit(solution)/shard_map/reduce_scatter | solution.py:218
  1313.4 6.4 fusion.73
  1322.6 41.7 %all-reduce.2 = (f32[768]{0:T(1024)}, f32[768]{0:T(1024)}, f32[768]{0:T(1024)}, f32[768]{0:T(1024)}, f32[]{:T(128)}, /*index=5*/f32[]{:T(128)}) all-reduce(f32[768]{0:T(1024)} %get-tuple-element.503, f32[768]{0:T(1024)} %get-tuple-element.506, f32[768]{0:T(1024)} %get-tuple-element.501, ...), channel_id=1, replica_groups=mesh['seq'=16,'batch'=2] {'seq','batch'}, use_global_device_ids=true, to_apply=%region_30.31 | all-reduce | flops 3074 | bytes 24592 | tf_op jit(solution)/shard_map/psum | solution.py:239
  1370.3 376.1 %all-reduce.6.cloned.1.call-done = (f32[768,2304]{1,0:T(8,128)}, f32[768,768]{1,0:T(8,128)}, f32[768,3072]{1,0:T(8,128)}, f32[3072,768]{1,0:T(8,128)}) async-done(((f32[768,2304]{1,0:T(8,128)}, f32[768,768]{1,0:T(8,128)}, f32[768,3072]{1,0:T(8,128)}, f32[3072,768]{1,0:T(8,128)}), (f32[768,2304]{1,0:T(8,128)}, f32[768,768]{1,0:T(8,128)}, f32[768,3072]{1,0:T(8,128)}, ...) | async-done | bytes 28311568 | tf_op jit(solution)/shard_map/psum | solution.py:239
  1746.4 6.6 copy.103
  1754.4 9.3 copy.105
  (550 shorter events, 507.2 us)
Async XLA Ops:
  7.2 162.6 %all-gather.4.cloned.1.call-start = ((), (), s32[]{:S(2)}) async-start(), calls=%async_computation.1 | async-start | bytes 13369344 | tf_op jit(solution)/shard_map/all_gather | solution.py:110
  14.9 1291.6 %reduce-scatter.2.cloned.1.call-start = ((), (), s32[]{:S(2)}) async-start(), calls=%async_computation.2 | async-start | bytes 26738688 | tf_op jit(solution)/shard_map/reduce_scatter | solution.py:218
  22.6 167.0 %copy-start.55 = (pred[256]{0:T(512)(128)(4,1)}, pred[256]{0:T(512)(128)(4,1)S(1)}, u32[]{:S(2)}) copy-start(pred[256]{0:T(512)(128)(4,1)S(1)} %broadcast_compare_fusion) | copy-start | bytes 772
  22.6 167.0 %copy-start.39 = (s32[256]{0:T(256)}, s32[256]{0:T(256)S(1)}, u32[]{:S(2)}) copy-start(s32[256]{0:T(256)S(1)} %iota_add_fusion) | copy-start | bytes 3076
  22.7 167.0 %copy-start.45 = (pred[4096]{0:T(1024)(128)(4,1)}, pred[4096]{0:T(1024)(128)(4,1)S(1)}, u32[]{:S(2)}) copy-start(pred[4096]{0:T(1024)(128)(4,1)S(1)} %iota_compare_fusion.8) | copy-start | bytes 12292
  483.5 10.0 copy-start.18
  483.5 10.0 copy-start.53
  483.8 9.8 copy-start.61
  483.8 7.4 slice-start.3
  531.5 6.7 copy-start.4
  556.1 6.7 copy-start.4
  580.7 6.7 copy-start.4
  605.3 6.7 copy-start.4
  629.9 6.7 copy-start.4
  654.6 6.7 copy-start.4
  679.1 6.7 copy-start.4
  752.8 6.7 copy-start.4
  777.4 6.7 copy-start.4
  793.5 32.5 %copy-start.41 = (s32[256]{0:T(256)}, s32[256]{0:T(256)S(1)}, u32[]{:S(2)}) copy-start(s32[256]{0:T(256)S(1)} %get-tuple-element.983) | copy-start | bytes 3076
  935.5 10.3 copy-start.23
  947.3 6.7 copy-start.43
  947.4 6.7 copy-start.48
  947.4 6.7 copy-start.54
  947.4 799.0 %all-reduce.6.cloned.1.call-start = ((), (), s32[]{:S(2)}) async-start(), calls=%async_computation.3 | async-start | bytes 56623104 | tf_op jit(solution)/shard_map/psum | solution.py:239
  959.5 349.6 %copy-start.44 = (f32[768]{0:T(1024)S(1)}, f32[768]{0:T(1024)}, u32[]{:S(2)}) copy-start(f32[768]{0:T(1024)} %param.21) | copy-start | bytes 9220
  959.5 349.6 %copy-start.49 = (f32[768]{0:T(1024)S(1)}, f32[768]{0:T(1024)}, u32[]{:S(2)}) copy-start(f32[768]{0:T(1024)} %param.22) | copy-start | bytes 9220
  959.5 349.6 %copy-start.52 = (f32[256]{0:T(256)S(1)}, f32[256]{0:T(256)}, u32[]{:S(2)}) copy-start(f32[256]{0:T(256)} %copy-done.51) | copy-start | bytes 3076
  959.5 349.6 %copy-start.60 = (f32[256]{0:T(256)S(1)}, f32[256]{0:T(256)}, u32[]{:S(2)}) copy-start(f32[256]{0:T(256)} %copy-done.59) | copy-start | bytes 3076
  1319.9 45.8 %copy-start.64 = (f32[256]{0:T(256)S(1)}, f32[256]{0:T(256)}, u32[]{:S(2)}) copy-start(f32[256]{0:T(256)} %copy-done.63) | copy-start | bytes 3076
  1752.9 10.7 slice-start
  1754.4 9.3 slice-start.1
  1754.4 9.3 slice-start.2
  (96 other events, 332.2 us)
Sparse Core Ops, SparseCore 0:
  15.0 154.7 all-gather.3
  947.5 359.0 reduce-scatter.1
  1314.1 432.2 all-reduce.5
where the time goes:
time: 1790 us; the launch traced here: 1780 us
  waiting for transfers between devices  864 us (48%)
  matrix products  346 us (19%)
  local copies, waits for them, and re-layouts  229 us (13%)
  other arithmetic  137 us (8%)
  blocking collectives  122 us (7%)
  loops' own time  58.8 us (3%)
  between operations  18.8 us (1%)
    psum x1, waiting for transfers between devices, per_device(): lax.psum((grad_w_qkv, grad_w_out, grad_ln1_gain, grad_ln1_bias, grad_w_up...  376 us
    reduce_scatter x1, waiting for transfers between devices, per_device(): lax.psum_scatter(kv_store, 'seq', scatter_dimension=1, tiled=True)  341 us
    dot_general x39, matrix products, contract_cols(): lax.dot_general(left_op, right_op, (((1,), (1,)), ((), ())), preferred_el...  187 us
    all_gather x1, waiting for transfers between devices, per_device(): lax.all_gather(projected[:, model_width:], 'seq', axis=0, tiled=True)  147 us
    dot_general x12, matrix products, attend(): jnp.dot(prob_low, value_head, preferred_element_type=jnp.float32)  53.6 us
    dot_general x28, matrix products, contract_rows(): lax.dot_general(left_op, right_op, (((0,), (0,)), ((), ())), preferred_el...  52.6 us
    all_gather x1, blocking collectives, prefix(): everything = lax.all_gather(shard, axis)  41.8 us
    psum x1, blocking collectives, per_device(): lax.psum((grad_w_qkv, grad_w_out, grad_ln1_gain, grad_ln1_bias, grad_w_up...  41.7 us
  transfers between devices with their start and end apart: 3, of which 3 were waited for; matrix products, arithmetic and copies ran while one was open for 2% of the time, Pallas kernels for 0%

commit v1 on v0

v1 whole, which is shorter than its diff:
```python
import functools

import jax
import jax.numpy as jnp
from jax import lax
from jax.experimental import pallas as pl
from jax.experimental.pallas import tpu as pltpu
from jax.sharding import PartitionSpec as P

HEADS = 12
HEAD_DIM = 64
TEAMS = 4
TEAM_HEADS = HEADS // TEAMS
TEAM_WIDTH = TEAM_HEADS * HEAD_DIM
QUERY_WIDTH = TEAM_WIDTH + HEAD_DIM

epsilon = 1e-05
negative = -1e30
select_scale = 3.0
VMEM_BYTES = 60 * 2**20
MESH = pl.DeviceIdType.MESH


def peers_of(scope):
    count = lax.axis_size("seq")
    lanes = count // TEAMS
    me = lax.axis_index("seq")
    team, lane = me // lanes, lax.rem(me, lanes)
    if scope == "team":
        return lane, lanes, lambda k: team * lanes + k
    if scope == "lane":
        return team, TEAMS, lambda k: k * lanes + lane
    return me, count, lambda k: k


def exchange(scope, kinds, arrays, collective):
    number = len(arrays)

    def body(*refs):
        sources, targets = refs[:number], refs[number : 2 * number]
        send, receive, local = refs[2 * number :]
        mine, peers, index_of = peers_of(scope)
        barrier = pltpu.get_barrier_semaphore()
        for k in range(1, peers):
            pl.semaphore_signal(
                barrier,
                inc=1,
                device_id={"seq": index_of(lax.rem(mine + k, peers))},
                device_id_type=MESH,
            )
        pl.semaphore_wait(barrier, peers - 1)
        copies = []
        for k in range(1, peers):
            peer = lax.rem(mine + k, peers)
            for n in range(number):
                copy = pltpu.make_async_remote_copy(
                    src_ref=sources[n] if kinds[n] == "gather" else sources[n].at[peer],
                    dst_ref=targets[n].at[mine],
                    send_sem=send.at[n, k],
                    recv_sem=receive.at[n, k],
                    device_id={"seq": index_of(peer)},
                    device_id_type=MESH,
                )
                copy.start()
                copies.append(copy)
        for n in range(number):
            copy = pltpu.make_async_copy(
                sources[n] if kinds[n] == "gather" else sources[n].at[mine],
                targets[n].at[mine],
                local.at[n],
            )
            copy.start()
            copies.append(copy)
        for copy in copies:
            copy.wait()

    count = {"team": lax.axis_size("seq") // TEAMS, "lane": TEAMS, "all": lax.axis_size("seq")}[scope]
    shapes = [
        jax.ShapeDtypeStruct(((count,) if kind == "gather" else ()) + x.shape, x.dtype)
        for kind, x in zip(kinds, arrays)
    ]
    return pl.pallas_call(
        body,
        out_shape=shapes,
        in_specs=[pl.BlockSpec(memory_space=pl.ANY)] * number,
        out_specs=[pl.BlockSpec(memory_space=pl.ANY)] * number,
        scratch_shapes=[
            pltpu.SemaphoreType.DMA((number, count)),
            pltpu.SemaphoreType.DMA((number, count)),
            pltpu.SemaphoreType.DMA((number,)),
        ],
        compiler_params=pltpu.CompilerParams(
            collective_id=collective, has_side_effects=True, vmem_limit_bytes=VMEM_BYTES
        ),
    )(*arrays)


def dot(left, right):
    return jnp.dot(left, right, preferred_element_type=jnp.float32)


def attend_body(
    length_ref,
    threshold_ref,
    q_ref,
    kk_ref,
    vv_ref,
    out_ref,
    mass_ref,
    carried_ref,
    excess_ref,
    key_heads,
    value_rows,
    running,
    logits,
    *,
    blocks,
    rows,
):
    lanes = blocks // TEAMS
    me = lax.axis_index("seq")
    team, lane = me // lanes, lax.rem(me, lanes)
    i = pl.program_id(0)
    scale = select_scale / (blocks * rows)

    @pl.when(i == 0)
    def _():
        running[...] = jnp.zeros_like(running)
        excess_ref[...] = jnp.zeros_like(excess_ref)
        for z in range(TEAMS):
            for h in range(TEAM_HEADS + 1):
                key_heads[h, z] = kk_ref[z, :, h * HEAD_DIM : (h + 1) * HEAD_DIM]
            value_rows[z] = vv_ref[z].T

    active = jnp.where(i >= lane, (i - lane) // lanes + 1, 0)
    q_rows = q_ref[0, 0].T
    heads = [q_rows[h * HEAD_DIM : (h + 1) * HEAD_DIM] for h in range(TEAM_HEADS + 1)]
    key_iota = lax.broadcasted_iota(jnp.int32, (rows, rows), 0)
    query_iota = lax.broadcasted_iota(jnp.int32, (rows, rows), 1)
    earlier = (key_iota < query_iota).astype(jnp.bfloat16)
    ones = jnp.ones((rows, rows), jnp.bfloat16)
    query_pos = i * rows + query_iota
    query_valid = query_pos < length_ref[0]
    threshold = threshold_ref[0]

    def score(z, peaks):
        key_pos = (z * lanes + lane) * rows + key_iota
        first = dot(key_heads[TEAM_HEADS, z], heads[TEAM_HEADS])
        chosen = (key_pos < query_pos) & (key_pos >= 1)
        selected = jnp.where(chosen, jnp.maximum(first, 0.0) * scale, 0.0).astype(jnp.bfloat16)
        carried = running[z] + dot(selected, earlier)
        running[z] = running[z] + dot(selected, ones)

        @pl.when(lax.rem(i, TEAMS) == team)
        def _():
            clipped = jnp.where(
                chosen & query_valid, jnp.clip(carried - threshold, 0.0, 1.0), 0.0
            )
            excess_ref[...] += jnp.sum(clipped.reshape(rows // 8, 8, rows), axis=0)

        carried = jnp.where(key_pos <= query_pos, carried, -negative)
        carried_ref[0, z] = carried
        result = []
        for h in range(TEAM_HEADS):
            logit = dot(key_heads[h, z], heads[h]) - carried
            logits[h, z] = logit
            result.append(
                jnp.maximum(peaks[h], jnp.max(logit.reshape(rows // 8, 8, rows), axis=0))
            )
        return tuple(result)

    start = tuple(jnp.full((8, rows), negative, jnp.float32) for _ in range(TEAM_HEADS))
    peaks = lax.fori_loop(0, active, score, start)
    peaks = [jnp.max(peak, axis=0, keepdims=True) for peak in peaks]

    def gather_values(z, state):
        masses, mixed = state
        new_masses, new_mixed = [], []
        for h in range(TEAM_HEADS):
            terms = jnp.exp(logits[h, z] - peaks[h])
            new_masses.append(masses[h] + jnp.sum(terms.reshape(rows // 8, 8, rows), axis=0))
            values = value_rows[z, h * HEAD_DIM : (h + 1) * HEAD_DIM, :]
            new_mixed.append(mixed[h] + dot(values, terms.astype(jnp.bfloat16)))
        return tuple(new_masses), tuple(new_mixed)

    masses, mixed = lax.fori_loop(
        0,
        active,
        gather_values,
        (
            tuple(jnp.zeros((8, rows), jnp.float32) for _ in range(TEAM_HEADS)),
            tuple(jnp.zeros((HEAD_DIM, rows), jnp.float32) for _ in range(TEAM_HEADS)),
        ),
    )
    mass_ref[0] = jnp.zeros((8, rows), jnp.float32)
    for h in range(TEAM_HEADS):
        mass = jnp.sum(masses[h], axis=0, keepdims=True)
        mass = jnp.where(active > 0, mass, 1.0)
        out_ref[0, h * HEAD_DIM : (h + 1) * HEAD_DIM, :] = (mixed[h] * (1.0 / mass)).astype(
            jnp.bfloat16
        )
        mass_ref[0, h : h + 1, :] = jnp.where(
            active > 0, peaks[h] + jnp.log(mass), negative
        )


def attend(length, threshold, queries, keys, values, blocks, rows):
    lanes = blocks // TEAMS
    smem = pl.BlockSpec(memory_space=pltpu.SMEM)
    whole = pl.BlockSpec((TEAMS, rows, QUERY_WIDTH), lambda i: (0, 0, 0))
    return pl.pallas_call(
        functools.partial(attend_body, blocks=blocks, rows=rows),
        grid=(blocks,),
        in_specs=[
            smem,
            smem,
            pl.BlockSpec(
                (1, 1, rows, QUERY_WIDTH), lambda i: (lax.rem(i, lanes), i // lanes, 0, 0)
            ),
            whole,
            pl.BlockSpec((TEAMS, rows, TEAM_WIDTH), lambda i: (0, 0, 0)),
        ],
        out_specs=[
            pl.BlockSpec((1, TEAM_WIDTH, rows), lambda i: (i, 0, 0)),
            pl.BlockSpec((1, 8, rows), lambda i: (i, 0, 0)),
            pl.BlockSpec((1, TEAMS, rows, rows), lambda i: (i, 0, 0, 0)),
            pl.BlockSpec((8, rows), lambda i: (0, 0)),
        ],
        out_shape=[
            jax.ShapeDtypeStruct((blocks, TEAM_WIDTH, rows), jnp.bfloat16),
            jax.ShapeDtypeStruct((blocks, 8, rows), jnp.float32),
            jax.ShapeDtypeStruct((blocks, TEAMS, rows, rows), jnp.float32),
            jax.ShapeDtypeStruct((8, rows), jnp.float32),
        ],
        scratch_shapes=[
            pltpu.VMEM((TEAM_HEADS + 1, TEAMS, rows, HEAD_DIM), jnp.bfloat16),
            pltpu.VMEM((TEAMS, TEAM_WIDTH, rows), jnp.bfloat16),
            pltpu.VMEM((TEAMS, rows, rows), jnp.float32),
            pltpu.VMEM((TEAM_HEADS, TEAMS, rows, rows), jnp.float32),
        ],
        compiler_params=pltpu.CompilerParams(vmem_limit_bytes=VMEM_BYTES),
    )(length, threshold, queries, keys, values)


def attend_back_body(
    q_ref,
    grad_ref,
    stat_ref,
    carried_ref,
    kk_ref,
    vv_ref,
    query_grad_ref,
    key_grad_ref,
    value_grad_ref,
    key_heads,
    key_rows,
    value_heads,
    running,
    key_sum,
    value_sum,
    *,
    blocks,
    rows,
):
    lanes = blocks // TEAMS
    lane = lax.rem(lax.axis_index("seq"), lanes)
    step = pl.program_id(0)
    i = blocks - 1 - step
    scale = select_scale / (blocks * rows)

    @pl.when(step == 0)
    def _():
        running[...] = jnp.zeros_like(running)
        key_sum[...] = jnp.zeros_like(key_sum)
        value_sum[...] = jnp.zeros_like(value_sum)
        for z in range(TEAMS):
            for h in range(TEAM_HEADS + 1):
                key_heads[h, z] = kk_ref[z, :, h * HEAD_DIM : (h + 1) * HEAD_DIM]
            for h in range(TEAM_HEADS):
                value_heads[h, z] = vv_ref[z, :, h * HEAD_DIM : (h + 1) * HEAD_DIM]
            key_rows[z] = kk_ref[z].T

    active = jnp.where(i >= lane, (i - lane) // lanes + 1, 0)
    q_rows = q_ref[0, 0].T
    grad_rows = grad_ref[0, 0].T
    span = [slice(h * HEAD_DIM, (h + 1) * HEAD_DIM) for h in range(TEAM_HEADS + 1)]
    q_row = [q_rows[span[h]] for h in range(TEAM_HEADS + 1)]
    q_col = [q_ref[0, 0, :, span[h]] for h in range(TEAM_HEADS + 1)]
    grad_row = [grad_rows[span[h]] for h in range(TEAM_HEADS)]
    grad_col = [grad_ref[0, 0, :, span[h]] for h in range(TEAM_HEADS)]
    mass = [stat_ref[0, 0, h : h + 1, :] for h in range(TEAM_HEADS)]
    inner = [stat_ref[0, 0, TEAM_HEADS + h : TEAM_HEADS + h + 1, :] for h in range(TEAM_HEADS)]
    key_iota = lax.broadcasted_iota(jnp.int32, (rows, rows), 0)
    query_iota = lax.broadcasted_iota(jnp.int32, (rows, rows), 1)
    later = (key_iota > query_iota).astype(jnp.bfloat16)
    ones = jnp.ones((rows, rows), jnp.bfloat16)
    query_pos = i * rows + query_iota

    def back(z, query_sum):
        key_pos = (z * lanes + lane) * rows + key_iota
        carried = carried_ref[0, z]
        total = None
        new_sum = []
        for h in range(TEAM_HEADS):
            probs = jnp.exp(dot(key_heads[h, z], q_row[h]) - carried - mass[h])
            value_sum[h, z] += dot(probs.astype(jnp.bfloat16), grad_col[h])
            grad_logit = probs * (dot(value_heads[h, z], grad_row[h]) - inner[h])
            total = grad_logit if total is None else total + grad_logit
            low = grad_logit.astype(jnp.bfloat16)
            key_sum[h, z] += dot(low, q_col[h])
            new_sum.append(query_sum[h] + dot(key_rows[z, span[h], :], low))
        total = total.astype(jnp.bfloat16)
        select_grad = running[z] - dot(total, later)
        running[z] = running[z] - dot(total, ones)
        first = dot(key_heads[TEAM_HEADS, z], q_row[TEAM_HEADS])
        live = (key_pos < query_pos) & (key_pos >= 1) & (first > 0.0)
        low = jnp.where(live, select_grad * scale, 0.0).astype(jnp.bfloat16)
        key_sum[TEAM_HEADS, z] += dot(low, q_col[TEAM_HEADS])
        new_sum.append(query_sum[TEAM_HEADS] + dot(key_rows[z, span[TEAM_HEADS], :], low))
        return tuple(new_sum)

    query_sum = lax.fori_loop(
        0,
        active,
        back,
        tuple(jnp.zeros((HEAD_DIM, rows), jnp.float32) for _ in range(TEAM_HEADS + 1)),
    )
    for h in range(TEAM_HEADS + 1):
        query_grad_ref[0, span[h], :] = query_sum[h].astype(jnp.bfloat16)

    @pl.when(step == blocks - 1)
    def _():
        for h in range(TEAM_HEADS + 1):
            key_grad_ref[:, :, span[h]] = key_sum[h].astype(jnp.bfloat16)
        for h in range(TEAM_HEADS):
            value_grad_ref[:, :, span[h]] = value_sum[h].astype(jnp.bfloat16)


def attend_back(queries, grads, stats, carried, keys, values, blocks, rows):
    lanes = blocks // TEAMS

    def place(step):
        i = blocks - 1 - step
        return (lax.rem(i, lanes), i // lanes, 0, 0)

    return pl.pallas_call(
        functools.partial(attend_back_body, blocks=blocks, rows=rows),
        grid=(blocks,),
        in_specs=[
            pl.BlockSpec((1, 1, rows, QUERY_WIDTH), place),
            pl.BlockSpec((1, 1, rows, TEAM_WIDTH), place),
            pl.BlockSpec((1, 1, 8, rows), place),
            pl.BlockSpec((1, TEAMS, rows, rows), lambda step: (blocks - 1 - step, 0, 0, 0)),
            pl.BlockSpec((TEAMS, rows, QUERY_WIDTH), lambda step: (0, 0, 0)),
            pl.BlockSpec((TEAMS, rows, TEAM_WIDTH), lambda step: (0, 0, 0)),
        ],
        out_specs=[
            pl.BlockSpec((1, QUERY_WIDTH, rows), lambda step: (blocks - 1 - step, 0, 0)),
            pl.BlockSpec((TEAMS, rows, QUERY_WIDTH), lambda step: (0, 0, 0)),
            pl.BlockSpec((TEAMS, rows, TEAM_WIDTH), lambda step: (0, 0, 0)),
        ],
        out_shape=[
            jax.ShapeDtypeStruct((blocks, QUERY_WIDTH, rows), jnp.bfloat16),
            jax.ShapeDtypeStruct((TEAMS, rows, QUERY_WIDTH), jnp.bfloat16),
            jax.ShapeDtypeStruct((TEAMS, rows, TEAM_WIDTH), jnp.bfloat16),
        ],
        scratch_shapes=[
            pltpu.VMEM((TEAM_HEADS + 1, TEAMS, rows, HEAD_DIM), jnp.bfloat16),
            pltpu.VMEM((TEAMS, QUERY_WIDTH, rows), jnp.bfloat16),
            pltpu.VMEM((TEAM_HEADS, TEAMS, rows, HEAD_DIM), jnp.bfloat16),
            pltpu.VMEM((TEAMS, rows, rows), jnp.float32),
            pltpu.VMEM((TEAM_HEADS + 1, TEAMS, rows, HEAD_DIM), jnp.float32),
            pltpu.VMEM((TEAM_HEADS, TEAMS, rows, HEAD_DIM), jnp.float32),
        ],
        compiler_params=pltpu.CompilerParams(vmem_limit_bytes=VMEM_BYTES),
    )(queries, grads, stats, carried, keys, values)


def layer_norm(values, norm_gain, norm_bias):
    row_mean = jnp.mean(values, axis=-1, keepdims=True)
    centred = values - row_mean
    variance = jnp.mean(centred * centred, axis=-1, keepdims=True)
    return centred * lax.rsqrt(variance + epsilon) * norm_gain + norm_bias


def gelu_tanh(values):
    return jax.nn.gelu(values, approximate=True)


def contract_rows(left_op, right_op):
    return lax.dot_general(
        left_op, right_op, (((0,), (0,)), ((), ())), preferred_element_type=jnp.float32
    )


def contract_cols(left_op, right_op):
    return lax.dot_general(
        left_op, right_op, (((1,), (1,)), ((), ())), preferred_element_type=jnp.float32
    )


def per_device(
    block_input,
    ln1_gain,
    ln1_bias,
    w_qkv,
    w_out,
    ln2_gain,
    ln2_bias,
    w_up,
    w_down,
    length_draw,
    threshold_index,
    grad_out,
):
    rows = block_input.shape[1]
    width = block_input.shape[2]
    blocks = lax.axis_size("seq")
    lanes = blocks // TEAMS
    group_len = blocks * rows
    me = lax.axis_index("seq")
    team = me // lanes
    score_scale = HEAD_DIM ** (-0.5)
    length = group_len - rows + 1 + length_draw % rows
    row_valid = (me * rows + jnp.arange(rows, dtype=jnp.int32) < length[0])[:, None]
    threshold = threshold_index.astype(jnp.float32) / 128.0
    tokens = block_input[0]
    grad_top = grad_out[0]
    grad_top_low = grad_top.astype(jnp.bfloat16)

    normed, ln1_pull = jax.vjp(layer_norm, tokens, ln1_gain, ln1_bias)
    normed_low = normed.astype(jnp.bfloat16)
    (lane_rows,) = exchange("lane", ["gather"], [normed_low], 0)
    lane_rows = lane_rows.reshape(TEAMS * rows, width)

    def columns(part):
        return lax.dynamic_slice_in_dim(w_qkv, part * width + team * TEAM_WIDTH, TEAM_WIDTH, 1)

    query_weight = jnp.concatenate([columns(0), w_qkv[:, :HEAD_DIM]], axis=1)
    key_weight = jnp.concatenate([columns(1), w_qkv[:, width : width + HEAD_DIM]], axis=1)
    queries = (dot(lane_rows, query_weight).astype(jnp.bfloat16) * score_scale).astype(
        jnp.bfloat16
    )
    keys = dot(lane_rows, key_weight).astype(jnp.bfloat16).reshape(TEAMS, rows, QUERY_WIDTH)
    values = dot(lane_rows, columns(2)).astype(jnp.bfloat16).reshape(TEAMS, rows, TEAM_WIDTH)
    (queries,) = exchange("team", ["gather"], [queries.reshape(TEAMS, rows, QUERY_WIDTH)], 1)

    parts, masses, carried, excess = attend(
        length, threshold, queries, keys, values, blocks, rows
    )
    parts, masses = exchange("all", ["spread", "spread"], [parts, masses], 2)
    parts = parts.astype(jnp.float32).reshape(TEAMS, lanes, TEAM_HEADS, HEAD_DIM, rows)
    masses = masses.reshape(TEAMS, lanes, 8, rows)[:, :, :TEAM_HEADS]
    peak = jnp.max(masses, axis=1, keepdims=True)
    shares = jnp.exp(masses - peak)
    mass = jnp.sum(shares, axis=1, keepdims=True)
    shares = shares / mass
    log_mass = (peak + jnp.log(mass))[:, 0]
    head_out = jnp.sum(parts * shares[:, :, :, None, :], axis=1)
    attn_mixed = jnp.where(
        row_valid, head_out.reshape(width, rows).T, 0.0
    ).astype(jnp.bfloat16)

    residual = tokens + dot(attn_mixed, w_out)
    normed_two, ln2_pull = jax.vjp(layer_norm, residual, ln2_gain, ln2_bias)
    normed_two_low = normed_two.astype(jnp.bfloat16)
    hidden = dot(normed_two_low, w_up)
    activated, gelu_pull = jax.vjp(gelu_tanh, hidden)
    activated_low = activated.astype(jnp.bfloat16)
    layer_out = residual + dot(activated_low, w_down)
    grad_w_down = contract_rows(activated_low, grad_top_low)
    grad_hidden_low = gelu_pull(contract_cols(grad_top_low, w_down))[0].astype(jnp.bfloat16)
    grad_w_up = contract_rows(normed_two_low, grad_hidden_low)
    grad_resid_norm, grad_ln2_gain, grad_ln2_bias = ln2_pull(contract_cols(grad_hidden_low, w_up))
    grad_resid = grad_top + grad_resid_norm
    grad_attn_low = grad_resid.astype(jnp.bfloat16)
    grad_w_out = contract_rows(attn_mixed, grad_attn_low)
    grad_mixed = jnp.where(
        row_valid,
        contract_cols(grad_attn_low, w_out).astype(jnp.bfloat16),
        jnp.zeros((), jnp.bfloat16),
    )
    grad_w_down, grad_w_up, grad_w_out = lax.psum(
        (
            grad_w_down.astype(jnp.bfloat16),
            grad_w_up.astype(jnp.bfloat16),
            grad_w_out.astype(jnp.bfloat16),
        ),
        ("seq", "batch"),
    )

    grad_rows = grad_mixed.T.reshape(TEAMS, TEAM_HEADS, HEAD_DIM, rows).astype(jnp.float32)
    inner = jnp.sum(grad_rows * head_out, axis=2)
    stats = jnp.concatenate(
        [log_mass, inner, jnp.zeros((TEAMS, 8 - 2 * TEAM_HEADS, rows), jnp.float32)], axis=1
    )
    grad_cols = jnp.moveaxis(grad_mixed.reshape(rows, TEAMS, TEAM_WIDTH), 1, 0)
    grad_cols, stats = exchange("lane", ["spread", "spread"], [grad_cols, stats], 3)
    grad_cols, stats = exchange("team", ["gather", "gather"], [grad_cols, stats], 4)
    query_grads, key_grads, value_grads = attend_back(
        queries, grad_cols, stats, carried, keys, values, blocks, rows
    )
    (query_grads,) = exchange("all", ["spread"], [query_grads], 5)
    key_grads, value_grads = exchange("lane", ["spread", "spread"], [key_grads, value_grads], 6)

    query_grads = query_grads.astype(jnp.float32).reshape(TEAMS, lanes, QUERY_WIDTH, rows)
    query_grads = jnp.sum(query_grads, axis=1)
    grad_query = query_grads[:, :TEAM_WIDTH].reshape(width, rows)
    grad_query = grad_query.at[:HEAD_DIM].add(jnp.sum(query_grads[:, TEAM_WIDTH:], axis=0))
    grad_query = grad_query.T * score_scale
    key_grads = key_grads.astype(jnp.float32)
    grad_key = jnp.moveaxis(key_grads[:, :, :TEAM_WIDTH], 0, 1).reshape(rows, width)
    grad_key = grad_key.at[:, :HEAD_DIM].add(jnp.sum(key_grads[:, :, TEAM_WIDTH:], axis=0))
    grad_value = jnp.moveaxis(value_grads, 0, 1).reshape(rows, width)
    grad_qkv_low = jnp.concatenate(
        [grad_query.astype(jnp.bfloat16), grad_key.astype(jnp.bfloat16), grad_value], axis=1
    )
    grad_w_qkv = contract_rows(normed_low, grad_qkv_low)
    grad_tokens_norm, grad_ln1_gain, grad_ln1_bias = ln1_pull(contract_cols(grad_qkv_low, w_qkv))
    grad_x = grad_resid + grad_tokens_norm

    pairs = (length[0] - 1).astype(jnp.float32) * (length[0] - 2).astype(jnp.float32) / 2.0
    counts = jnp.stack([jnp.sum(excess), pairs / blocks])
    vectors = jnp.concatenate(
        [grad_ln1_gain, grad_ln1_bias, grad_ln2_gain, grad_ln2_bias, counts]
    )
    grad_w_qkv, vectors = lax.psum(
        (grad_w_qkv.astype(jnp.bfloat16), vectors), ("seq", "batch")
    )
    pruned_share = (vectors[4 * width] / vectors[4 * width + 1]).reshape(1)
    return (
        layer_out[None],
        grad_x[None],
        vectors[:width],
        vectors[width : 2 * width],
        grad_w_qkv.astype(jnp.float32),
        grad_w_out.astype(jnp.float32),
        vectors[2 * width : 3 * width],
        vectors[3 * width : 4 * width],
        grad_w_up.astype(jnp.float32),
        grad_w_down.astype(jnp.float32),
        pruned_share,
    )


def solution(mesh):
    placed = (
        P("batch", "seq", None),
        P(),
        P(),
        P(),
        P(),
        P(),
        P(),
        P(),
        P(),
        P("batch"),
        P(),
        P("batch", "seq", None),
    )
    return jax.shard_map(
        per_device,
        mesh=mesh,
        in_specs=placed,
        out_specs=(
            P("batch", "seq", None),
            P("batch", "seq", None),
            P(),
            P(),
            P(),
            P(),
            P(),
            P(),
            P(),
            P(),
            P(),
        ),
        check_vma=False,
    )
```

time: 1790 us -> 695 us (0.39)
  waiting for transfers between devices: 864 us -> 189 us
  Pallas kernels: 0 us -> 316 us
  matrix products: 346 us -> 42 us
  local copies, waits for them, and re-layouts: 229 us -> 25.9 us
  other arithmetic: 137 us -> 46.8 us
  blocking collectives: 122 us -> 55.5 us
  loops' own time: 58.8 us -> 0 us
    reduce_scatter x1 -> x0, waiting for transfers between devices: 341 us -> none  [per_device(): lax.psum_scatter(kv_store, 'seq', scatter_dimension=1, tiled=True)]
    pallas_call x0 -> x9, Pallas kernels: none -> 316 us  [the longest x7 209 us: exchange(): pl.pallas_call(body, out_shape=shapes, in_specs=[pl.BlockSpec(memory_spac...]
    psum x1, waiting for transfers between devices: 376 us -> 189 us  [per_device(): lax.psum((grad_w_qkv.astype(jnp.bfloat16), vectors), ('seq', 'batch'))]
    dot_general x39 -> x4, matrix products: 187 us -> 11.2 us  [contract_cols(): lax.dot_general(left_op, right_op, (((1,), (1,)), ((), ())), preferred_el...]
    all_gather x1 -> x0, waiting for transfers between devices: 147 us -> none  [per_device(): lax.all_gather(projected[:, model_width:], 'seq', axis=0, tiled=True)]
    dot_general x28 -> x6, matrix products: 107 us -> 17.1 us  [dot(): return jnp.dot(left, right, preferred_element_type=jnp.float32)]
    all_gather x2 -> x0, blocking collectives: 80.2 us -> none  [the longest x1 41.8 us: prefix(): everything = lax.all_gather(shard, axis)]
    another operation x4 -> x0, loops' own time: 58.8 us -> none  [the longest x1 29.3 us: per_device(): lax.scan(back_head, (-grad_first, kv_empty), jnp.arange(1, HEADS, dtype=j...]
  transfers between devices with their start and end apart: 3 -> 1, of which waited for: 3 -> 1; matrix products, arithmetic and copies ran while one was open for 2% -> 2% of each run, Pallas kernels for 0% -> 0%
where the time goes in v1:
time: 695 us; the launch traced here: 694 us
  Pallas kernels  316 us (45%)
  waiting for transfers between devices  189 us (27%)
  blocking collectives  55.5 us (8%)
  other arithmetic  46.8 us (7%)
  matrix products  42 us (6%)
  local copies, waits for them, and re-layouts  25.9 us (4%)
  between operations  18.9 us (3%)
    pallas_call x7, Pallas kernels, exchange(): pl.pallas_call(body, out_shape=shapes, in_specs=[pl.BlockSpec(memory_spac...  209 us
    psum x1, waiting for transfers between devices, per_device(): lax.psum((grad_w_qkv.astype(jnp.bfloat16), vectors), ('seq', 'batch'))  189 us
    pallas_call x1, Pallas kernels, attend_back(): pl.pallas_call(functools.partial(attend_back_body, blocks=blocks, rows=ro...  61.1 us
    psum x1, blocking collectives, per_device(): lax.psum((grad_w_qkv.astype(jnp.bfloat16), vectors), ('seq', 'batch'))  55.5 us
    pallas_call x1, Pallas kernels, attend(): pl.pallas_call(functools.partial(attend_body, blocks=blocks, rows=rows),...  45 us
    dot_general x6, matrix products, dot(): return jnp.dot(left, right, preferred_element_type=jnp.float32)  17.1 us
  transfers between devices with their start and end apart: 1, of which 1 were waited for; matrix products, arithmetic and copies ran while one was open for 2% of the time, Pallas kernels for 0%

profile of v1, /device:TPU:0, one launch (start us, length us, event | category | flops | bytes accessed | tf_op | source)
XLA Modules:
  0.0 693.8 jit_solution(13250464996240944911)
XLA Ops:
  11.3 2.1 add_convert_fusion.1.refs_0_
  13.4 31.7 %shard_map.203 = bf16[4,256,768]{2,1,0:T(8,128)(2,1)} custom-call(bf16[256,768]{1,0:T(8,128)(2,1)} %add_convert_fusion.1.refs_0_), custom_call_target="tpu_custom_call" | custom-call | tf_op jit(solution)/shard_map/pallas_call | solution.py:82
  48.6 3.0 fusion.9
  51.6 26.4 %shard_map.204.q_ref = bf16[4,4,256,256]{3,2,1,0:T(8,128)(2,1)} custom-call(bf16[4,256,256]{2,1,0:T(8,128)(2,1)} %bitcast.106), custom_call_target="tpu_custom_call" | custom-call | tf_op jit(solution)/shard_map/pallas_call | solution.py:82
  80.9 2.4 convolution_convert_fusion.4
  83.2 45.0 %shard_map.205 = (bf16[16,192,256]{2,1,0:T(8,128)(2,1)}, f32[16,8,256]{2,1,0:T(8,128)}, f32[16,4,256,256]{3,2,1,0:T(8,128)}, f32[8,256]{1,0:T(8,128)}) custom-call(s32[1]{0:T(128)} %add.123.length_ref, f32[1]{0:T(128)S(6)} %div.63.threshold_ref, bf16[4,4,256,256]{3,2,1,0:T(8,128)(2,1)} %shard_map.204.q_ref, bf16[4,256,256]{2,1,0:T(8,128)(2,1)} %bitcast.102, ...), custom_call_target="tpu_custom_call" | custom-call | tf_op jit(solution)/shard_map/pallas_call | solution.py:211
  128.2 38.1 %shard_map.206 = (bf16[16,192,256]{2,1,0:T(8,128)(2,1)}, f32[16,8,256]{2,1,0:T(8,128)}) custom-call(bf16[16,192,256]{2,1,0:T(8,128)(2,1)} %get-tuple-element.50.refs_0_, f32[16,8,256]{2,1,0:T(8,128)} %get-tuple-element.51.refs_1_), custom_call_target="tpu_custom_call" | custom-call | tf_op jit(solution)/shard_map/pallas_call | solution.py:82
  169.1 1.9 fusion.7
  173.7 4.0 fusion.34
  177.7 3.0 fusion.6
  180.8 2.3 multiply_reduce_fusion
  186.1 1.9 convert_bitcast_fusion
  190.4 2.3 copy.33
  194.7 21.3 %shard_map.207 = (bf16[4,256,192]{2,1,0:T(8,128)(2,1)}, f32[4,8,256]{2,1,0:T(8,128)}) custom-call(bf16[4,256,192]{2,1,0:T(8,128)(2,1)} %bitcast.101, f32[4,8,256]{2,1,0:T(8,128)} %maximum_maximum_fusion.refs_1_), custom_call_target="tpu_custom_call" | custom-call | tf_op jit(solution)/shard_map/pallas_call | solution.py:82
  216.1 28.7 %shard_map.208 = (bf16[4,4,256,192]{3,2,1,0:T(8,128)(2,1)}, f32[4,4,8,256]{3,2,1,0:T(8,128)}) custom-call(bf16[4,256,192]{2,1,0:T(8,128)(2,1)} %get-tuple-element.54.refs_0_, f32[4,8,256]{2,1,0:T(8,128)} %get-tuple-element.55.refs_1_), custom_call_target="tpu_custom_call" | custom-call | tf_op jit(solution)/shard_map/pallas_call | solution.py:82
  244.9 61.1 %shard_map.209 = (bf16[16,256,256]{2,1,0:T(8,128)(2,1)}, bf16[4,256,256]{2,1,0:T(8,128)(2,1)}, bf16[4,256,192]{2,1,0:T(8,128)(2,1)}) custom-call(bf16[4,4,256,256]{3,2,1,0:T(8,128)(2,1)} %shard_map.204.q_ref, bf16[4,4,256,192]{3,2,1,0:T(8,128)(2,1)} %get-tuple-element.56.grad_ref, f32[4,4,8,256]{3,2,1,0:T(8,128)} %get-tuple-element.57.stat_ref, ...), custom_call_target="tpu_custom_call" | custom-call | tf_op jit(solution)/shard_map/pallas_call | solution.py:346
  305.9 23.7 %shard_map.211 = (bf16[4,256,256]{2,1,0:T(8,128)(2,1)}, bf16[4,256,192]{2,1,0:T(8,128)(2,1)}) custom-call(bf16[4,256,256]{2,1,0:T(8,128)(2,1)} %get-tuple-element.60.refs_0_, bf16[4,256,192]{2,1,0:T(8,128)(2,1)} %get-tuple-element.61.refs_1_), custom_call_target="tpu_custom_call" | custom-call | tf_op jit(solution)/shard_map/pallas_call | solution.py:82
  333.4 39.4 %shard_map.210 = bf16[16,256,256]{2,1,0:T(8,128)(2,1)} custom-call(bf16[16,256,256]{2,1,0:T(8,128)(2,1)} %get-tuple-element.59.refs_0_), custom_call_target="tpu_custom_call" | custom-call | tf_op jit(solution)/shard_map/pallas_call | solution.py:82
  372.9 2.1 convert_reduce_fusion
  377.3 3.8 convolution_convert_fusion.1
  381.1 4.5 convolution_convert_fusion
  385.5 2.1 copy.37
  387.6 2.4 copy.34
  393.1 2.3 add_select_fusion
  401.4 3.9 convolution_convert_fusion.2
  406.9 4.7 multiply_reduce_fusion.1
  413.0 55.5 %psum.35 = f32[3074]{0:T(1024)S(1)} all-reduce(f32[3074]{0:T(1024)S(1)} %concatenate.23), channel_id=1, replica_groups=mesh['seq'=16,'batch'=2] {'seq','batch'}, use_global_device_ids=true, to_apply=%region_21.22 | all-reduce | flops 3074 | bytes 24592 | tf_op jit(solution)/shard_map/psum | solution.py:527
  474.6 5.4 fusion.8
  480.0 189.1 %all-reduce.3.cloned.1.call-done = (bf16[768,2304]{1,0:T(8,128)(2,1)}, bf16[768,768]{1,0:T(8,128)(2,1)}, bf16[768,3072]{1,0:T(8,128)(2,1)}, bf16[3072,768]{1,0:T(8,128)(2,1)}) async-done(((bf16[768,2304]{1,0:T(8,128)(2,1)}, bf16[768,768]{1,0:T(8,128)(2,1)}, bf16[768,3072]{1,0:T(8,128)(2,1)}, bf16[3072,768]{1,0:T(8,128)(2,1)}), (bf16[768,2304]{1,0:T(8,128)(2,1)}, bf16[768,768]{1,0:T(8,128)(2,1)}, ...) | async-done | bytes 14155792 | tf_op jit(solution)/shard_map/psum | solution.py:527
  669.1 5.6 convert_element_type.114
  676.3 5.0 convert_element_type.118
  681.4 4.5 convert_element_type.120
  (155 shorter events, 45.6 us)
Async XLA Ops:
  7.2 165.6 %copy-start = (bf16[768,768]{1,0:T(8,128)(2,1)S(1)}, bf16[768,768]{1,0:T(8,128)(2,1)}, u32[]{:S(2)}) copy-start(bf16[768,768]{1,0:T(8,128)(2,1)} %param.20) | copy-start | bytes 3538948
  7.2 661.9 %all-reduce.3.cloned.1.call-start = ((), (), s32[]{:S(2)}) async-start(), calls=%async_computation | async-start | bytes 28311552 | tf_op jit(solution)/shard_map/psum | solution.py:527
  9.9 37.1 %copy-start.29 = (f32[256]{0:T(256)}, f32[256]{0:T(256)S(1)}, u32[]{:S(2)}) copy-start(f32[256]{0:T(256)S(1)} %broadcast_multiply_fusion.1) | copy-start | bytes 3076
  11.3 35.7 %copy-start.35 = (f32[256]{0:T(256)}, f32[256]{0:T(256)S(1)}, u32[]{:S(2)}) copy-start(f32[256]{0:T(256)S(1)} %multiply_reduce_fusion.6) | copy-start | bytes 3076
  11.3 35.7 %copy-start.33 = (f32[256]{0:T(256)}, f32[256]{0:T(256)S(1)}, u32[]{:S(2)}) copy-start(f32[256]{0:T(256)S(1)} %fusion.28) | copy-start | bytes 3076
  48.6 29.4 %copy-start.5 = (bf16[4,256,768]{2,1,0:T(8,128)(2,1)S(1)}, bf16[4,256,768]{2,1,0:T(8,128)(2,1)}, u32[]{:S(2)}) copy-start(bf16[4,256,768]{2,1,0:T(8,128)(2,1)} %shard_map.203) | copy-start | bytes 4718596
  128.2 44.6 %copy-start.2 = (f32[1,256,768]{2,1,0:T(8,128)S(1)}, f32[1,256,768]{2,1,0:T(8,128)}, u32[]{:S(2)}) copy-start(f32[1,256,768]{2,1,0:T(8,128)} %param.16) | copy-start | bytes 2359300
  173.4 9.7 %copy-start.26 = (f32[256]{0:T(256)}, f32[256]{0:T(256)S(1)}, u32[]{:S(2)}) copy-start(f32[256]{0:T(256)S(1)} %broadcast_multiply_fusion) | copy-start | bytes 3076
  173.4 4.3 slice-start.7
  173.7 9.4 %copy-start.31 = (f32[256]{0:T(256)}, f32[256]{0:T(256)S(1)}, u32[]{:S(2)}) copy-start(f32[256]{0:T(256)S(1)} %fusion.29) | copy-start | bytes 3076
  173.7 4.0 copy-start.13
  173.7 4.0 slice-start.8
  173.7 7.0 %slice-start.5 = ((s8[4718592]{0:T(1024)(128)(4,1)}), s8[4194304]{0:T(1024)(128)(4,1)S(1)}, s32[]{:S(2)}) async-start(s8[4718592]{0:T(1024)(128)(4,1)} %bitcast.113), calls=%async_computation.6 | async-start | bytes 8388608
  184.9 7.8 %copy-start.4 = (f32[4,3,64,256]{3,2,1,0:T(8,128)S(1)}, f32[4,3,64,256]{3,2,1,0:T(8,128)}, u32[]{:S(2)}) copy-start(f32[4,3,64,256]{3,2,1,0:T(8,128)} %copy-done.3) | copy-start | bytes 2359300
  189.4 4.7 copy-start.25
  372.9 4.4 copy-start.11
  372.9 4.4 copy-start.22
  372.9 4.4 copy-start.24
  372.9 4.4 copy-start.27
  372.9 4.4 copy-start.32
  375.0 6.0 copy-start.6
  377.3 3.8 copy-start.14
  385.5 14.2 %slice-start.4 = ((f32[4,256,256]{2,1,0:T(8,128)}), f32[4,192,256]{2,1,0:T(8,128)S(1)}, s32[]{:S(2)}) async-start(f32[4,256,256]{2,1,0:T(8,128)} %copy-done.6), calls=%async_computation.5 | async-start | bytes 1572864 | tf_op jit(solution)/shard_map/slice | solution.py:508
  385.5 15.9 %copy-start.9 = (bf16[256,768]{1,0:T(8,128)(2,1)S(1)}, bf16[256,768]{1,0:T(8,128)(2,1)}, u32[]{:S(2)}) copy-start(bf16[256,768]{1,0:T(8,128)(2,1)} %add_convert_fusion.1.refs_0_) | copy-start | bytes 1179652
  406.9 63.9 %copy-start.36 = (f32[256]{0:T(256)S(1)}, f32[256]{0:T(256)}, u32[]{:S(2)}) copy-start(f32[256]{0:T(256)} %copy-done.35) | copy-start | bytes 3076
  468.6 6.1 copy-start.39
  669.1 7.2 %slice-start.2 = ((s8[4718592]{0:T(1024)(128)(4,1)}), s8[4194304]{0:T(1024)(128)(4,1)S(1)}, s32[]{:S(2)}) async-start(s8[4718592]{0:T(1024)(128)(4,1)} %bitcast.93), calls=%async_computation.3 | async-start | bytes 8388608
  669.1 5.6 copy-start.12
  669.1 7.2 %slice-start.3 = ((s8[4718592]{0:T(1024)(128)(4,1)}), s8[524288]{0:T(1024)(128)(4,1)S(1)}, s32[]{:S(2)}) async-start(s8[4718592]{0:T(1024)(128)(4,1)} %bitcast.93), calls=%async_computation.4 | async-start | bytes 1048576
  674.7 6.6 slice-start
  676.3 5.1 slice-start.1
  681.4 4.5 copy-start.1
  (18 other events, 35.4 us)
Sparse Core Ops, SparseCore 0:
  405.6 263.4 all-reduce.2

commit v2 on v1

--- a/solution.py
+++ b/solution.py
@@ -326,7 +326,7 @@
         tuple(jnp.zeros((HEAD_DIM, rows), jnp.float32) for _ in range(TEAM_HEADS + 1)),
     )
     for h in range(TEAM_HEADS + 1):
-        query_grad_ref[0, span[h], :] = query_sum[h].astype(jnp.bfloat16)
+        query_grad_ref[0, 0, span[h], :] = query_sum[h].astype(jnp.bfloat16)
 
     @pl.when(step == blocks - 1)
     def _():
@@ -355,12 +355,12 @@
             pl.BlockSpec((TEAMS, rows, TEAM_WIDTH), lambda step: (0, 0, 0)),
         ],
         out_specs=[
-            pl.BlockSpec((1, QUERY_WIDTH, rows), lambda step: (blocks - 1 - step, 0, 0)),
+            pl.BlockSpec((1, 1, QUERY_WIDTH, rows), place),
             pl.BlockSpec((TEAMS, rows, QUERY_WIDTH), lambda step: (0, 0, 0)),
             pl.BlockSpec((TEAMS, rows, TEAM_WIDTH), lambda step: (0, 0, 0)),
         ],
         out_shape=[
-            jax.ShapeDtypeStruct((blocks, QUERY_WIDTH, rows), jnp.bfloat16),
+            jax.ShapeDtypeStruct((lanes, TEAMS, QUERY_WIDTH, rows), jnp.bfloat16),
             jax.ShapeDtypeStruct((TEAMS, rows, QUERY_WIDTH), jnp.bfloat16),
             jax.ShapeDtypeStruct((TEAMS, rows, TEAM_WIDTH), jnp.bfloat16),
         ],
@@ -374,6 +374,232 @@
         ],
         compiler_params=pltpu.CompilerParams(vmem_limit_bytes=VMEM_BYTES),
     )(queries, grads, stats, carried, keys, values)
+
+
+def finish_body(
+    main_ref,
+    extra_ref,
+    rows_ref,
+    vector_ref,
+    whole_ref,
+    home_ref,
+    total_ref,
+    core_main,
+    core_extra,
+    send_main,
+    send_extra,
+    lane_main,
+    lane_extra,
+    team_send_main,
+    team_send_extra,
+    team_main,
+    team_extra,
+    assembled,
+    vectors,
+    ready,
+    core_sems,
+    lane_sems,
+    team_sems,
+    home_sems,
+    vector_sems,
+    out_lane_sems,
+    out_core_send,
+    out_core_recv,
+    local_sems,
+):
+    blocks = lax.axis_size("seq")
+    lanes = blocks // TEAMS
+    me = lax.axis_index("seq")
+    core = lax.axis_index("batch")
+    team, lane = me // lanes, lax.rem(me, lanes)
+
+    def lane_peer(k):
+        other = lax.rem(lane + k, lanes)
+        return other, {"seq": team * lanes + other}
+
+    def team_peer(k):
+        other = lax.rem(team + k, TEAMS)
+        return other, {"seq": other * lanes + lane}
+
+    sibling = {"batch": 1 - core}
+    barrier = pltpu.get_barrier_semaphore()
+    targets = [sibling]
+    targets += [lane_peer(k)[1] for k in range(1, lanes)]
+    targets += [team_peer(k)[1] for k in range(1, TEAMS)]
+    for target in targets:
+        pl.semaphore_signal(barrier, inc=1, device_id=target, device_id_type=MESH)
+    pl.semaphore_wait(barrier, len(targets))
+
+    def push(source, destination, send, receive, target):
+        copy = pltpu.make_async_remote_copy(
+            src_ref=source,
+            dst_ref=destination,
+            send_sem=send,
+            recv_sem=receive,
+            device_id=target,
+            device_id_type=MESH,
+        )
+        copy.start()
+        return copy
+
+    theirs = pl.ds((1 - core) * lanes, lanes)
+    core_copies = [
+        push(main_ref.at[theirs], core_main, core_sems.at[0, 0], core_sems.at[1, 0], sibling),
+        push(extra_ref.at[theirs], core_extra, core_sems.at[0, 1], core_sems.at[1, 1], sibling),
+        push(vector_ref, vectors.at[0], vector_sems.at[0, 0], vector_sems.at[1, 0], sibling),
+    ]
+    home_copies = []
+    for k in range(1, TEAMS):
+        other, target = team_peer(k)
+        home_copies.append(
+            push(rows_ref.at[other], home_ref.at[team], home_sems.at[0, k], home_sems.at[1, k], target)
+        )
+    own = pltpu.make_async_copy(rows_ref.at[team], home_ref.at[team], local_sems.at[0])
+    own.start()
+    for copy in core_copies:
+        copy.wait()
+
+    both = vector_ref[...] + vectors[0]
+    vectors[1 + lane] = both
+    ready[0] = both
+    for j in range(lanes):
+        send_main[j] = (
+            main_ref[core * lanes + j].astype(jnp.float32) + core_main[j].astype(jnp.float32)
+        ).astype(jnp.bfloat16)
+        send_extra[j] = (
+            extra_ref[core * lanes + j].astype(jnp.float32) + core_extra[j].astype(jnp.float32)
+        ).astype(jnp.bfloat16)
+    lane_copies = []
+    for k in range(1, lanes):
+        other, target = lane_peer(k)
+        lane_copies += [
+            push(send_main.at[other], lane_main.at[lane], lane_sems.at[0, 0, k], lane_sems.at[1, 0, k], target),
+            push(send_extra.at[other], lane_extra.at[lane], lane_sems.at[0, 1, k], lane_sems.at[1, 1, k], target),
+            push(ready.at[0], vectors.at[1 + lane], vector_sems.at[0, k], vector_sems.at[1, k], target),
+        ]
+    lane_main[lane] = send_main[lane]
+    lane_extra[lane] = send_extra[lane]
+    for copy in lane_copies:
+        copy.wait()
+
+    def total(ref, start, number):
+        result = ref[start].astype(jnp.float32)
+        for j in range(1, number):
+            result = result + ref[start + j].astype(jnp.float32)
+        return result
+
+    whole_vector = total(vectors, 1, lanes)
+    ready[1] = whole_vector
+    vectors[1 + lanes + team] = whole_vector
+    low_main = total(lane_main, 0, lanes).astype(jnp.bfloat16)
+    low_extra = total(lane_extra, 0, lanes).astype(jnp.bfloat16)
+    team_send_main[...] = low_main
+    team_send_extra[...] = low_extra
+    team_main[team] = low_main
+    team_extra[team] = low_extra
+    team_copies = []
+    for k in range(1, TEAMS):
+        other, target = team_peer(k)
+        at = lanes + k
+        team_copies += [
+            push(team_send_main, team_main.at[team], team_sems.at[0, 0, k], team_sems.at[1, 0, k], target),
+            push(team_send_extra, team_extra.at[team], team_sems.at[0, 1, k], team_sems.at[1, 1, k], target),
+            push(ready.at[1], vectors.at[1 + lanes + team], vector_sems.at[0, at], vector_sems.at[1, at], target),
+        ]
+    for copy in team_copies:
+        copy.wait()
+    total_ref[...] = total(vectors, 1 + lanes, TEAMS)
+    extra = total(team_extra, 0, TEAMS)
+    pieces = []
+    for part in range(3):
+        for g in range(TEAMS):
+            piece = team_main[g, :, part * TEAM_WIDTH : (part + 1) * TEAM_WIDTH]
+            if g == 0 and part < 2:
+                more = extra[:, part * HEAD_DIM : (part + 1) * HEAD_DIM]
+                first = (piece[:, :HEAD_DIM].astype(jnp.float32) + more).astype(jnp.bfloat16)
+                pieces += [first, piece[:, HEAD_DIM:]]
+            else:
+                pieces.append(piece)
+    assembled[...] = jnp.concatenate(pieces, axis=1)
+
+    mine = core * lanes + lane
+    out_copies = []
+    for k in range(1, lanes):
+        _, target = lane_peer(k)
+        out_copies.append(
+            push(assembled, whole_ref.at[mine], out_lane_sems.at[0, k], out_lane_sems.at[1, k], target)
+        )
+    core_out = [
+        push(assembled, whole_ref.at[mine], out_core_send.at[0], out_core_recv.at[0], sibling)
+    ]
+    kept = pltpu.make_async_copy(assembled, whole_ref.at[mine], local_sems.at[1])
+    kept.start()
+    for k in range(1, lanes):
+        source = core * lanes + lax.rem(lane - k + lanes, lanes)
+        out_copies[k - 1].wait_recv()
+        core_out.append(
+            push(whole_ref.at[source], whole_ref.at[source], out_core_send.at[k], out_core_recv.at[k], sibling)
+        )
+    for copy in out_copies:
+        copy.wait_send()
+    for copy in core_out + home_copies:
+        copy.wait()
+    own.wait()
+    kept.wait()
+
+
+def finish(main, extra, rows_out, vector, collective):
+    lanes = lax.axis_size("seq") // TEAMS
+    chunks, depth, main_width = main.shape
+    extra_width = extra.shape[2]
+    low = jnp.bfloat16
+    dma = pltpu.SemaphoreType.DMA
+    return pl.pallas_call(
+        finish_body,
+        out_shape=[
+            jax.ShapeDtypeStruct((chunks, depth, TEAMS * main_width), low),
+            jax.ShapeDtypeStruct(rows_out.shape, low),
+            jax.ShapeDtypeStruct(vector.shape, jnp.float32),
+        ],
+        in_specs=[
+            pl.BlockSpec(memory_space=pltpu.VMEM),
+            pl.BlockSpec(memory_space=pltpu.VMEM),
+            pl.BlockSpec(memory_space=pl.ANY),
+            pl.BlockSpec(memory_space=pltpu.VMEM),
+        ],
+        out_specs=[
+            pl.BlockSpec(memory_space=pl.ANY),
+            pl.BlockSpec(memory_space=pl.ANY),
+            pl.BlockSpec(memory_space=pltpu.VMEM),
+        ],
+        scratch_shapes=[
+            pltpu.VMEM((lanes, depth, main_width), low),
+            pltpu.VMEM((lanes, depth, extra_width), low),
+            pltpu.VMEM((lanes, depth, main_width), low),
+            pltpu.VMEM((lanes, depth, extra_width), low),
+            pltpu.VMEM((lanes, depth, main_width), low),
+            pltpu.VMEM((lanes, depth, extra_width), low),
+            pltpu.VMEM((depth, main_width), low),
+            pltpu.VMEM((depth, extra_width), low),
+            pltpu.VMEM((TEAMS, depth, main_width), low),
+            pltpu.VMEM((TEAMS, depth, extra_width), low),
+            pltpu.VMEM((depth, TEAMS * main_width), low),
+            pltpu.VMEM((1 + lanes + TEAMS,) + vector.shape, jnp.float32),
+            pltpu.VMEM((2,) + vector.shape, jnp.float32),
+            dma((2, 2)),
+            dma((2, 2, lanes)),
+            dma((2, 2, TEAMS)),
+            dma((2, TEAMS)),
+            dma((2, lanes + TEAMS)),
+            dma((2, lanes)),
+            dma((lanes,)),
+            dma((lanes,)),
+            dma((2,)),
+        ],
+        compiler_params=pltpu.CompilerParams(
+            collective_id=collective, has_side_effects=True, vmem_limit_bytes=VMEM_BYTES
+        ),
+    )(main, extra, rows_out, vector)
 
 
 def layer_norm(values, norm_gain, norm_bias):
@@ -436,13 +662,17 @@
     def columns(part):
         return lax.dynamic_slice_in_dim(w_qkv, part * width + team * TEAM_WIDTH, TEAM_WIDTH, 1)
 
-    query_weight = jnp.concatenate([columns(0), w_qkv[:, :HEAD_DIM]], axis=1)
-    key_weight = jnp.concatenate([columns(1), w_qkv[:, width : width + HEAD_DIM]], axis=1)
-    queries = (dot(lane_rows, query_weight).astype(jnp.bfloat16) * score_scale).astype(
-        jnp.bfloat16
-    )
-    keys = dot(lane_rows, key_weight).astype(jnp.bfloat16).reshape(TEAMS, rows, QUERY_WIDTH)
-    values = dot(lane_rows, columns(2)).astype(jnp.bfloat16).reshape(TEAMS, rows, TEAM_WIDTH)
+    team_weight = jnp.concatenate(
+        [columns(0), columns(1), columns(2), w_qkv[:, :HEAD_DIM], w_qkv[:, width : width + HEAD_DIM]],
+        axis=1,
+    )
+    projected = dot(lane_rows, team_weight).astype(jnp.bfloat16)
+    query_part, key_part, value_part, query_first, key_first = jnp.split(
+        projected, [TEAM_WIDTH, 2 * TEAM_WIDTH, 3 * TEAM_WIDTH, 3 * TEAM_WIDTH + HEAD_DIM], axis=1
+    )
+    queries = jnp.concatenate([query_part, query_first], axis=1) * jnp.bfloat16(score_scale)
+    keys = jnp.concatenate([key_part, key_first], axis=1).reshape(TEAMS, rows, QUERY_WIDTH)
+    values = value_part.reshape(TEAMS, rows, TEAM_WIDTH)
     (queries,) = exchange("team", ["gather"], [queries.reshape(TEAMS, rows, QUERY_WIDTH)], 1)
 
     parts, masses, carried, excess = attend(
@@ -500,43 +730,60 @@
     query_grads, key_grads, value_grads = attend_back(
         queries, grad_cols, stats, carried, keys, values, blocks, rows
     )
-    (query_grads,) = exchange("all", ["spread"], [query_grads], 5)
-    key_grads, value_grads = exchange("lane", ["spread", "spread"], [key_grads, value_grads], 6)
-
-    query_grads = query_grads.astype(jnp.float32).reshape(TEAMS, lanes, QUERY_WIDTH, rows)
-    query_grads = jnp.sum(query_grads, axis=1)
-    grad_query = query_grads[:, :TEAM_WIDTH].reshape(width, rows)
-    grad_query = grad_query.at[:HEAD_DIM].add(jnp.sum(query_grads[:, TEAM_WIDTH:], axis=0))
-    grad_query = grad_query.T * score_scale
-    key_grads = key_grads.astype(jnp.float32)
-    grad_key = jnp.moveaxis(key_grads[:, :, :TEAM_WIDTH], 0, 1).reshape(rows, width)
-    grad_key = grad_key.at[:, :HEAD_DIM].add(jnp.sum(key_grads[:, :, TEAM_WIDTH:], axis=0))
-    grad_value = jnp.moveaxis(value_grads, 0, 1).reshape(rows, width)
-    grad_qkv_low = jnp.concatenate(
-        [grad_query.astype(jnp.bfloat16), grad_key.astype(jnp.bfloat16), grad_value], axis=1
-    )
-    grad_w_qkv = contract_rows(normed_low, grad_qkv_low)
-    grad_tokens_norm, grad_ln1_gain, grad_ln1_bias = ln1_pull(contract_cols(grad_qkv_low, w_qkv))
-    grad_x = grad_resid + grad_tokens_norm
-
+    (query_grads,) = exchange("team", ["spread"], [query_grads], 5)
+    query_grads = jnp.sum(query_grads.astype(jnp.float32), axis=0) * score_scale
+    query_grads = jnp.swapaxes(query_grads.astype(jnp.bfloat16), 1, 2)
+    grad_projected = jnp.concatenate(
+        [
+            query_grads[:, :, :TEAM_WIDTH],
+            key_grads[:, :, :TEAM_WIDTH],
+            value_grads,
+            query_grads[:, :, TEAM_WIDTH:],
+            key_grads[:, :, TEAM_WIDTH:],
+        ],
+        axis=2,
+    ).reshape(TEAMS * rows, -1)
+    chunks = 2 * lanes
+    grad_main = contract_rows(lane_rows, grad_projected[:, : 3 * TEAM_WIDTH])
+    grad_extra = contract_rows(lane_rows, grad_projected[:, 3 * TEAM_WIDTH :])
+    grad_lane_rows = contract_cols(grad_projected, team_weight)
+    grad_ln1_bias = jnp.sum(grad_lane_rows, axis=0)
+    grad_ln1_gain = (
+        jnp.sum(grad_lane_rows * (lane_rows.astype(jnp.float32) - ln1_bias), axis=0) / ln1_gain
+    )
     pairs = (length[0] - 1).astype(jnp.float32) * (length[0] - 2).astype(jnp.float32) / 2.0
-    counts = jnp.stack([jnp.sum(excess), pairs / blocks])
-    vectors = jnp.concatenate(
-        [grad_ln1_gain, grad_ln1_bias, grad_ln2_gain, grad_ln2_bias, counts]
-    )
-    grad_w_qkv, vectors = lax.psum(
-        (grad_w_qkv.astype(jnp.bfloat16), vectors), ("seq", "batch")
-    )
-    pruned_share = (vectors[4 * width] / vectors[4 * width + 1]).reshape(1)
+    vectors = jnp.stack(
+        [
+            grad_ln1_gain,
+            grad_ln1_bias,
+            grad_ln2_gain,
+            grad_ln2_bias,
+            jnp.full((width,), jnp.sum(excess)),
+            jnp.full((width,), pairs / blocks),
+            jnp.zeros((width,), jnp.float32),
+            jnp.zeros((width,), jnp.float32),
+        ]
+    )
+    grad_w_qkv, home_rows, vectors = finish(
+        grad_main.astype(jnp.bfloat16).reshape(chunks, width // chunks, -1),
+        grad_extra.astype(jnp.bfloat16).reshape(chunks, width // chunks, -1),
+        grad_lane_rows.astype(jnp.bfloat16).reshape(TEAMS, rows, width),
+        vectors,
+        6,
+    )
+    grad_w_qkv = grad_w_qkv.reshape(width, 3 * width)
+    grad_normed = jnp.sum(home_rows.astype(jnp.float32), axis=0)
+    grad_x = grad_resid + ln1_pull(grad_normed)[0]
+    pruned_share = (vectors[4, 0] / vectors[5, 0]).reshape(1)
     return (
         layer_out[None],
         grad_x[None],
-        vectors[:width],
-        vectors[width : 2 * width],
+        vectors[0],
+        vectors[1],
         grad_w_qkv.astype(jnp.float32),
         grad_w_out.astype(jnp.float32),
-        vectors[2 * width : 3 * width],
-        vectors[3 * width : 4 * width],
+        vectors[2],
+        vectors[3],
         grad_w_up.astype(jnp.float32),
         grad_w_down.astype(jnp.float32),
         pruned_share,

time: 695 us -> 534 us (0.77); the launches traced: 694 us -> 525 us
  waiting for transfers between devices: 189 us -> 0.02 us
  Pallas kernels: 316 us -> 393 us
  blocking collectives: 55.5 us -> 0 us
    psum x1, waiting for transfers between devices: 189 us -> 0.01 us  [per_device(): lax.psum((grad_w_down.astype(jnp.bfloat16), grad_w_up.astype(jnp.bfloat16...]
    pallas_call x0 -> x1, Pallas kernels: none -> 102 us  [finish(): pl.pallas_call(finish_body, out_shape=[jax.ShapeDtypeStruct((chunks, dept...]
    psum x1 -> x0, blocking collectives: 55.5 us -> none  [per_device(): lax.psum((grad_w_qkv.astype(jnp.bfloat16), vectors), ('seq', 'batch'))]
    pallas_call x7 -> x6, Pallas kernels: 209 us -> 184 us  [exchange(): pl.pallas_call(body, out_shape=shapes, in_specs=[pl.BlockSpec(memory_spac...]
    dot_general x6 -> x4, matrix products: 17.1 us -> 12.5 us  [dot(): return jnp.dot(left, right, preferred_element_type=jnp.float32)]
    dot_general x4 -> x5, matrix products: 13.6 us -> 16.6 us  [contract_rows(): lax.dot_general(left_op, right_op, (((0,), (0,)), ((), ())), preferred_el...]
  transfers between devices with their start and end apart: 1 -> 1, of which waited for: 1 -> 0; matrix products, arithmetic and copies ran while one was open for 2% -> 10% of each run, Pallas kernels for 0% -> 48%
where the time goes in v2:
time: 534 us; the launch traced here: 525 us
  Pallas kernels  393 us (74%)
  matrix products  41.1 us (8%)
  other arithmetic  41 us (8%)
  local copies, waits for them, and re-layouts  31 us (6%)
  between operations  18.5 us (3%)
    pallas_call x6, Pallas kernels, exchange(): pl.pallas_call(body, out_shape=shapes, in_specs=[pl.BlockSpec(memory_spac...  184 us
    pallas_call x1, Pallas kernels, finish(): pl.pallas_call(finish_body, out_shape=[jax.ShapeDtypeStruct((chunks, dept...  102 us
    pallas_call x1, Pallas kernels, attend_back(): pl.pallas_call(functools.partial(attend_back_body, blocks=blocks, rows=ro...  61.2 us
    pallas_call x1, Pallas kernels, attend(): pl.pallas_call(functools.partial(attend_body, blocks=blocks, rows=rows),...  45 us
    dot_general x5, matrix products, contract_rows(): lax.dot_general(left_op, right_op, (((0,), (0,)), ((), ())), preferred_el...  16.6 us
    dot_general x4, matrix products, dot(): return jnp.dot(left, right, preferred_element_type=jnp.float32)  12.5 us
    dot_general x4, matrix products, contract_cols(): lax.dot_general(left_op, right_op, (((1,), (1,)), ((), ())), preferred_el...  12 us
  transfers between devices with their start and end apart: 1, of which 0 were waited for; matrix products, arithmetic and copies ran while one was open for 10% of the time, Pallas kernels for 48%

profile of v2, /device:TPU:0, one launch (start us, length us, event | category | flops | bytes accessed | tf_op | source)
XLA Modules:
  0.0 524.5 jit_solution(10664340676033232255)
XLA Ops:
  11.8 2.1 add_convert_fusion.1.refs_0_
  13.9 31.7 %shard_map.203 = bf16[4,256,768]{2,1,0:T(8,128)(2,1)} custom-call(bf16[256,768]{1,0:T(8,128)(2,1)} %add_convert_fusion.1.refs_0_), custom_call_target="tpu_custom_call" | custom-call | tf_op jit(solution)/shard_map/pallas_call | solution.py:82
  47.6 2.7 constant_dynamic-slice_fusion
  50.3 3.3 concatenate.20
  53.6 2.6 convolution_convert_fusion.2
  58.3 26.4 %shard_map.204.q_ref = bf16[4,4,256,256]{3,2,1,0:T(8,128)(2,1)} custom-call(bf16[4,256,256]{2,1,0:T(8,128)(2,1)} %maximum_multiply_fusion.refs_0_), custom_call_target="tpu_custom_call" | custom-call | tf_op jit(solution)/shard_map/pallas_call | solution.py:82
  86.8 45.0 %shard_map.205 = (bf16[16,192,256]{2,1,0:T(8,128)(2,1)}, f32[16,8,256]{2,1,0:T(8,128)}, f32[16,4,256,256]{3,2,1,0:T(8,128)}, f32[8,256]{1,0:T(8,128)}) custom-call(s32[1]{0:T(128)} %add.105.length_ref, f32[1]{0:T(128)S(6)} %div.66.threshold_ref, bf16[4,4,256,256]{3,2,1,0:T(8,128)(2,1)} %shard_map.204.q_ref, bf16[4,256,256]{2,1,0:T(8,128)(2,1)} %bitcast.92, ...), custom_call_target="tpu_custom_call" | custom-call | tf_op jit(solution)/shard_map/pallas_call | solution.py:211
  131.8 38.1 %shard_map.206 = (bf16[16,192,256]{2,1,0:T(8,128)(2,1)}, f32[16,8,256]{2,1,0:T(8,128)}) custom-call(bf16[16,192,256]{2,1,0:T(8,128)(2,1)} %get-tuple-element.27.refs_0_, f32[16,8,256]{2,1,0:T(8,128)} %get-tuple-element.28.refs_1_), custom_call_target="tpu_custom_call" | custom-call | tf_op jit(solution)/shard_map/pallas_call | solution.py:82
  177.0 4.0 fusion.21
  181.0 3.1 fusion.6
  184.2 2.2 multiply_reduce_fusion.2
  186.4 3.8 convolution_convert_fusion.1
  190.1 4.4 convolution_convert_fusion
  196.7 1.9 fusion.10
  199.9 1.9 convert_bitcast_fusion
  202.8 2.3 copy.42
  207.1 24.3 %shard_map.207 = (bf16[4,256,192]{2,1,0:T(8,128)(2,1)}, f32[4,8,256]{2,1,0:T(8,128)}) custom-call(bf16[4,256,192]{2,1,0:T(8,128)(2,1)} %bitcast.97, f32[4,8,256]{2,1,0:T(8,128)} %maximum_maximum_fusion.refs_1_), custom_call_target="tpu_custom_call" | custom-call | tf_op jit(solution)/shard_map/pallas_call | solution.py:82
  231.4 37.0 %shard_map.208 = (bf16[4,4,256,192]{3,2,1,0:T(8,128)(2,1)}, f32[4,4,8,256]{3,2,1,0:T(8,128)}) custom-call(bf16[4,256,192]{2,1,0:T(8,128)(2,1)} %get-tuple-element.31.refs_0_, f32[4,8,256]{2,1,0:T(8,128)} %get-tuple-element.32.refs_1_), custom_call_target="tpu_custom_call" | custom-call | tf_op jit(solution)/shard_map/pallas_call | solution.py:82
  268.4 61.2 %shard_map.209 = (bf16[4,4,256,256]{3,2,1,0:T(8,128)(2,1)}, bf16[4,256,256]{2,1,0:T(8,128)(2,1)}, bf16[4,256,192]{2,1,0:T(8,128)(2,1)}) custom-call(bf16[4,4,256,256]{3,2,1,0:T(8,128)(2,1)} %shard_map.204.q_ref, bf16[4,4,256,192]{3,2,1,0:T(8,128)(2,1)} %get-tuple-element.33.grad_ref, f32[4,4,8,256]{3,2,1,0:T(8,128)} %get-tuple-element.34.stat_ref, ...), custom_call_target="tpu_custom_call" | custom-call | tf_op jit(solution)/shard_map/pallas_call | solution.py:346
  329.6 26.9 %shard_map.210 = bf16[4,4,256,256]{3,2,1,0:T(8,128)(2,1)} custom-call(bf16[4,4,256,256]{3,2,1,0:T(8,128)(2,1)} %get-tuple-element.36.refs_0_), custom_call_target="tpu_custom_call" | custom-call | tf_op jit(solution)/shard_map/pallas_call | solution.py:82
  356.5 2.0 convert_reduce_fusion
  362.4 3.8 concatenate.26
  366.2 3.9 convolution_convert_fusion.4
  370.1 2.2 copy.44
  372.4 4.8 fusion.22
  379.2 2.9 convolution_convert_fusion.6
  382.1 102.3 %shard_map.211 = (bf16[8,96,2304]{2,1,0:T(8,128)(2,1)}, bf16[4,256,768]{2,1,0:T(8,128)(2,1)}, f32[8,768]{1,0:T(8,128)}) custom-call(bf16[8,96,576]{2,1,0:T(8,128)(2,1)} %bitcast.94, bf16[8,96,128]{2,1,0:T(8,128)(2,1)} %bitcast.113, bf16[4,256,768]{2,1,0:T(8,128)(2,1)} %bitcast.107, f32[8,768]{1,0:T(8,128)} %stack.17.vector_ref), custom_call_target="tpu_custom_call" | custom-call | tf_op jit(solution)/shard_map/pallas_call | solution.py:557
  492.6 5.4 %fusion.9 = f32[1,256,768]{2,1,0:T(8,128)} fusion(f32[256,768]{1,0:T(8,128)S(1)} %get-tuple-element.73, bf16[3072,768]{1,0:T(8,128)(2,1)} %param.20, f32[256,3072]{1,0:T(8,128)S(1)} %copy-done.26), kind=kOutput, calls=%fused_computation.24 | convolution fusion | flops 1215234048 | bytes 9437184 | tf_op jit(solution)/shard_map/dot_general | solution.py:99
  497.9 3.7 bitcast_convert_fusion
  501.6 3.0 convert_element_type.124
  504.6 7.4 %convert_element_type.126 = f32[768,3072]{1,0:T(8,128)} convert(bf16[768,3072]{1,0:T(8,128)(2,1)} %get-tuple-element.53) | non-fusion elementwise | flops 2359296 | bytes 14155776 | tf_op jit(solution)/shard_map/convert_element_type | solution.py:787
  512.1 4.5 convert_element_type.128
  (129 shorter events, 35.2 us)
Async XLA Ops:
  7.2 168.9 %copy-start = (bf16[768,768]{1,0:T(8,128)(2,1)S(1)}, bf16[768,768]{1,0:T(8,128)(2,1)}, u32[]{:S(2)}) copy-start(bf16[768,768]{1,0:T(8,128)(2,1)} %param.16) | copy-start | bytes 3538948
  7.2 494.4 %all-reduce.3.cloned.1.call-start = ((), (), s32[]{:S(2)}) async-start(), calls=%async_computation | async-start | bytes 21233664 | tf_op jit(solution)/shard_map/psum | solution.py:713
  9.3 2.0 copy-start.14
  10.6 0.6 copy-start.18
  45.6 8.0 %copy-start.6 = (bf16[4,256,768]{2,1,0:T(8,128)(2,1)S(1)}, bf16[4,256,768]{2,1,0:T(8,128)(2,1)}, u32[]{:S(2)}) copy-start(bf16[4,256,768]{2,1,0:T(8,128)(2,1)} %shard_map.203) | copy-start | bytes 4718596
  131.8 44.3 %copy-start.2 = (f32[1,256,768]{2,1,0:T(8,128)S(1)}, f32[1,256,768]{2,1,0:T(8,128)}, u32[]{:S(2)}) copy-start(f32[1,256,768]{2,1,0:T(8,128)} %param.12) | copy-start | bytes 2359300
  171.8 2.9 copy-start.9
  174.6 0.9 copy-start.3
  174.6 2.3 copy-start.11
  174.6 2.3 copy-start.12
  176.7 4.3 slice-start.4
  177.0 4.0 copy-start.8
  177.0 4.0 slice-start.5
  177.0 7.2 %slice-start.2 = ((s8[4718592]{0:T(1024)(128)(4,1)}), s8[4194304]{0:T(1024)(128)(4,1)S(1)}, s32[]{:S(2)}) async-start(s8[4718592]{0:T(1024)(128)(4,1)} %bitcast.114), calls=%async_computation.3 | async-start | bytes 8388608
  181.0 9.2 %copy-start.25 = (f32[256,3072]{1,0:T(8,128)}, f32[256,3072]{1,0:T(8,128)S(1)}, u32[]{:S(2)}) copy-start(f32[256,3072]{1,0:T(8,128)S(1)} %fusion.21) | copy-start | bytes 9437188
  181.0 3.2 slice-start.3
  198.6 6.5 %copy-start.4 = (f32[4,3,64,256]{3,2,1,0:T(8,128)S(1)}, f32[4,3,64,256]{3,2,1,0:T(8,128)}, u32[]{:S(2)}) copy-start(f32[4,3,64,256]{3,2,1,0:T(8,128)} %copy-done.3) | copy-start | bytes 2359300
  202.8 3.6 copy-start.10
  366.2 6.2 %copy-start.7 = (bf16[768,704]{1,0:T(8,128)(2,1)S(1)}, bf16[768,704]{1,0:T(8,128)(2,1)}, u32[]{:S(2)}) copy-start(bf16[768,704]{1,0:T(8,128)(2,1)} %concatenate.20) | copy-start | bytes 3244036
  366.2 6.2 %copy-start.21 = (f32[768]{0:T(1024)S(1)}, f32[768]{0:T(1024)}, u32[]{:S(2)}) copy-start(f32[768]{0:T(1024)} %param.14) | copy-start | bytes 9220
  372.4 4.8 copy-start.13
  372.4 4.8 copy-start.23
  372.4 4.8 copy-start.22
  372.4 4.8 copy-start.20
  379.2 111.2 %copy-start.15 = (f32[256]{0:T(256)S(1)}, f32[256]{0:T(256)}, u32[]{:S(2)}) copy-start(f32[256]{0:T(256)} %copy-done.14) | copy-start | bytes 3076
  382.1 108.5 %copy-start.19 = (f32[256]{0:T(256)S(1)}, f32[256]{0:T(256)}, u32[]{:S(2)}) copy-start(f32[256]{0:T(256)} %copy-done.18) | copy-start | bytes 3076
  382.1 108.5 %copy-start.17 = (f32[256]{0:T(256)S(1)}, f32[256]{0:T(256)}, u32[]{:S(2)}) copy-start(f32[256]{0:T(256)} %copy-done.16) | copy-start | bytes 3076
  490.3 2.2 copy-start.26
  492.5 5.4 %copy-start.5 = (bf16[8,96,2304]{2,1,0:T(8,128)(2,1)S(1)}, bf16[8,96,2304]{2,1,0:T(8,128)(2,1)}, u32[]{:S(2)}) copy-start(bf16[8,96,2304]{2,1,0:T(8,128)(2,1)} %get-tuple-element.42) | copy-start | bytes 10616836
  501.6 10.4 %slice-start = ((s8[4718592]{0:T(1024)(128)(4,1)}), s8[4194304]{0:T(1024)(128)(4,1)S(1)}, s32[]{:S(2)}) async-start(s8[4718592]{0:T(1024)(128)(4,1)} %bitcast.88), calls=%async_computation.1 | async-start | bytes 8388608
  504.6 7.4 %slice-start.1 = ((s8[4718592]{0:T(1024)(128)(4,1)}), s8[524288]{0:T(1024)(128)(4,1)S(1)}, s32[]{:S(2)}) async-start(s8[4718592]{0:T(1024)(128)(4,1)} %bitcast.88), calls=%async_computation.2 | async-start | bytes 1048576
  512.1 4.5 copy-start.1
  (2 other events, 1.1 us)
Sparse Core Ops, SparseCore 0:
  196.8 303.5 all-reduce.2
